TPU v7x, 32 devices: a whole 2x2x4 slice. The times are simulated.
32 devices in a mesh: dp: 4 (over z), mp: 2 (over core), section: 4 (over y, x).
Axes of the slice: x: 2, y: 2, z: 4, core: 2. Of those that a mesh axis runs over, the one named last changes fastest.
Arguments:
- states: bfloat16 [4096, 8192], P(('dp', 'section'), 'mp'), may hold values from -6 to 6
- direction: bfloat16 [4096, 256], P(('dp', 'section'), 'mp'), may hold values from -0.1875 to 0.1875
- old_logp: bfloat16 [4096], P(('dp', 'section')), may hold values from -4 to -0.049804688
- lengths: int32 [32], P(('dp', 'section')), may hold values from 1 to 128, as said below
- group_ids: int32 [32], P(('dp', 'section')), may hold values from 0 to 3, as said below
- routes: int32 [4096, 1], P(('dp', 'section')), may hold values from 0 to 3; in each aligned block of 256 rows (0 to 255, 256 to 511, ...) at most 80 rows name the same one
- reward_head: bfloat16 [8192], P('mp'), may hold values from -0.0625 to 0.0625
- policy_k: bfloat16 [8192, 256], P(('dp', 'section'), 'mp'), may hold values from -0.0625 to 0.0625
- reference_k: bfloat16 [8192, 256], P(('dp', 'section'), 'mp'), may hold values from -0.0625 to 0.0625
Outputs:
- grad_k: float32 [8192, 256], P(('dp', 'section'), 'mp')
- packed_logp: float32 [4, 4, 320], P('dp', 'section')
Inputs may be any that keep to these rules, and one draw needn't show every extreme that they name: `lengths`: some response has all 128 tokens valid. `group_ids`: each prompt id is held by exactly 8 responses. `routes`: among the rows of one rollout device at most 80 name the same learner shard, a bound that some block reaches of them.
All inputs are finite; a program needn't handle non-finite values.
Results may differ from a plain program's by a relative error of at most 0.004.
Values may be sent and summed in bfloat16 or wider, within the bound.
A program may use at most 64 MiB of HBM per device.

v0:
```python
import jax
import jax.numpy as jnp
from jax import lax
from jax.sharding import PartitionSpec as P

GROUP = 8


kl_weight = 0.4
var_offset = 0.25


def row_slots(routes, shards, capacity):
    target = routes[:, 0]
    choose = (target[:, None] == jnp.arange(shards, dtype=jnp.int32)[None, :]).astype(jnp.int32)
    ranked = jnp.cumsum(choose, axis=0) - 1
    within = jnp.sum(ranked * choose, axis=1)
    places = target * capacity + within
    row_count = routes.shape[0]
    source = jnp.full((shards * capacity,), row_count, jnp.int32)
    return source.at[places].set(jnp.arange(row_count, dtype=jnp.int32))


def pick_rows(values, source):
    return jnp.take(values, source, axis=0, mode="fill", fill_value=0)


def advantages(scores, lengths, group_ids):
    seq_count = lengths.shape[0]
    seq_len = scores.shape[0] // seq_count
    groups = seq_count * lax.axis_size("dp") * lax.axis_size("section") // GROUP
    valid = (jnp.arange(seq_len, dtype=jnp.int32)[None, :] < lengths[:, None]).astype(jnp.float32)
    reward = jnp.sum(scores.reshape(seq_count, seq_len) * valid, axis=1) / jnp.sqrt(
        lengths.astype(jnp.float32)
    )
    member = (group_ids[:, None] == jnp.arange(groups, dtype=jnp.int32)[None, :]).astype(
        jnp.float32
    )
    totals, squares = lax.psum(
        (
            jnp.sum(member * reward[:, None], axis=0),
            jnp.sum(member * (reward * reward)[:, None], axis=0),
        ),
        ("dp", "section"),
    )
    center = totals / GROUP
    spread = squares / GROUP - center * center
    own_center = jnp.sum(member * center[None, :], axis=1)
    own_spread = jnp.sum(member * spread[None, :], axis=1)
    advantage = ((reward - own_center) / jnp.sqrt(own_spread + var_offset)).astype(jnp.bfloat16)
    return (jnp.repeat(advantage, seq_len), valid.reshape(-1))


def project(whole, policy_k, reference_k):
    return (
        jnp.dot(
            whole,
            lax.all_gather(policy_k, ("dp", "section"), axis=0, tiled=True),
            preferred_element_type=jnp.float32,
        ),
        jnp.dot(
            whole,
            lax.all_gather(reference_k, ("dp", "section"), axis=0, tiled=True),
            preferred_element_type=jnp.float32,
        ),
    )


def token_coef(dir_rows, old_rows, adv_rows, valid_rows, term_policy, term_reference):
    logp = old_rows.astype(jnp.float32) + term_policy
    coef = valid_rows * (
        -adv_rows * jnp.exp(term_policy) + kl_weight * (1.0 - jnp.exp(term_reference - term_policy))
    )
    change = (coef[:, None] * dir_rows.astype(jnp.float32)).astype(jnp.bfloat16)
    return (logp, change)


def weight_grads(whole, change):
    return lax.psum_scatter(
        lax.dot_general(
            whole, change, (((0,), (0,)), ((), ())), preferred_element_type=jnp.float32
        ),
        ("dp", "section"),
        scatter_dimension=0,
        tiled=True,
    )


def body(
    states, direction, old_logp, lengths, group_ids, routes, reward_head, policy_k, reference_k
):
    row_count = states.shape[0]
    score_part = jnp.dot(states, reward_head, preferred_element_type=jnp.float32)
    shards = lax.axis_size("dp")
    capacity = max(2, 5 * row_count // (4 * shards))
    source = row_slots(routes, shards, capacity)
    scores = lax.psum(score_part, "mp")
    adv_rows, valid_rows = advantages(scores, lengths, group_ids)
    extras = jnp.stack([old_logp, adv_rows, valid_rows.astype(jnp.bfloat16)], axis=1)
    send_states = pick_rows(states, source).reshape(shards, capacity, states.shape[1])
    send_dir = pick_rows(direction, source).reshape(shards, capacity, direction.shape[1])
    send_extras = pick_rows(extras, source).reshape(shards, capacity, 3)
    got_states, got_dir, got_extras = (
        lax.all_to_all(send_states, "dp", split_axis=0, concat_axis=0, tiled=True),
        lax.all_to_all(send_dir, "dp", split_axis=0, concat_axis=0, tiled=True),
        lax.all_to_all(send_extras, "dp", split_axis=0, concat_axis=0, tiled=True),
    )
    slot_count = shards * capacity
    learn_states = got_states.reshape(slot_count, states.shape[1])
    learn_dir = got_dir.reshape(slot_count, direction.shape[1])
    learn_extras = got_extras.reshape(slot_count, 3)
    whole = lax.all_gather(learn_states, "mp", axis=1, tiled=True)
    key_policy, key_reference = project(whole, policy_k, reference_k)
    dir_wide = learn_dir.astype(jnp.float32)
    term_policy, term_reference = lax.psum(
        (jnp.sum(dir_wide * key_policy, axis=1), jnp.sum(dir_wide * key_reference, axis=1)), "mp"
    )
    logp, change = token_coef(
        learn_dir,
        learn_extras[:, 0],
        learn_extras[:, 1].astype(jnp.float32),
        learn_extras[:, 2].astype(jnp.float32),
        term_policy,
        term_reference,
    )
    grad_k = weight_grads(whole, change)
    packed_logp = logp.reshape(1, 1, slot_count)
    return (grad_k, packed_logp)


def solution(mesh):
    return jax.shard_map(
        body,
        mesh=mesh,
        in_specs=(
            P(("dp", "section"), "mp"),
            P(("dp", "section"), "mp"),
            P(("dp", "section")),
            P(("dp", "section")),
            P(("dp", "section")),
            P(("dp", "section"), None),
            P("mp"),
            P(("dp", "section"), "mp"),
            P(("dp", "section"), "mp"),
        ),
        out_specs=(P(("dp", "section"), "mp"), P("dp", "section", None)),
        check_vma=False,
    )
```

profile of v0, /device:TPU:0, one launch (start us, length us, event | category | flops | bytes accessed | tf_op | source)
XLA Modules:
  0.0 360.2 jit_solution(5305597054967255320)
XLA Ops:
  7.2 0.8 compare_convert_fusion
  8.0 1.2 reduce-window.6
  9.6 0.7 fusion.7
  10.3 0.7 compare_select_fusion
  11.0 1.4 scatter_custom_fusion
  12.5 3.9 %gather_fusion = bf16[320,4096]{1,0:T(8,128)(2,1)} fusion(bf16[256,4096]{1,0:T(8,128)(2,1)S(1)} %copy-done, s32[1024]{0:T(1024)S(1)} %pad_clamp_fusion), kind=kCustom, calls=%fused_computation | custom fusion | bytes 5244160 | tf_op jit(solution)/shard_map/jit(_take)/gather | solution.py:25
  16.4 3.5 broadcast_select_fusion
  19.9 6.3 %all-to-all-start = ((bf16[4,80,4096]{2,1,0:T(8,128)(2,1)}), bf16[4,80,4096]{2,1,0:T(8,128)(2,1)}, u32[]{:S(2)}, u32[]{:S(2)}) async-start(bf16[4,80,4096]{2,1,0:T(8,128)(2,1)} %broadcast_select_fusion), calls=%async_computation | async-start | bytes 5242880 | tf_op jit(solution)/shard_map/all_to_all | solution.py:104
  27.0 65.3 %all-to-all-done = bf16[4,80,4096]{2,1,0:T(8,128)(2,1)} async-done(((bf16[4,80,4096]{2,1,0:T(8,128)(2,1)}), bf16[4,80,4096]{2,1,0:T(8,128)(2,1)}, u32[]{:S(2)}, u32[]{:S(2)}) %all-to-all-start) | async-done | bytes 2621472 | tf_op jit(solution)/shard_map/all_to_all | solution.py:104
  93.1 1.4 gather_fusion.2
  94.5 0.7 broadcast_select_fusion.1
  95.2 3.3 all-to-all-start.2
  99.3 5.1 %all-to-all-done.2 = bf16[4,80,128]{2,1,0:T(8,128)(2,1)S(1)} async-done(((bf16[4,80,128]{2,1,0:T(8,128)(2,1)}), bf16[4,80,128]{2,1,0:T(8,128)(2,1)S(1)}, u32[]{:S(2)}, u32[]{:S(2)}) %all-to-all-start.2) | async-done | bytes 81952 | tf_op jit(solution)/shard_map/all_to_all | solution.py:105
  104.4 14.0 %all-gather.6.cloned.1.call-done = bf16[8192,128]{1,0:T(8,128)(2,1)} async-done(((bf16[512,128]{1,0:T(8,128)(2,1)}), bf16[8192,128]{1,0:T(8,128)(2,1)}) %all-gather.6.cloned.1.call-update) | async-done | bytes 2097168 | tf_op jit(solution)/shard_map/all_gather | solution.py:58
  118.4 15.4 %all-gather.4.cloned.1.call-done = bf16[320,8192]{1,0:T(8,128)(2,1)} async-done(((bf16[320,4096]{1,0:T(8,128)(2,1)}), bf16[320,8192]{1,0:T(8,128)(2,1)}) %all-gather.4.cloned.1.call-update) | async-done | bytes 5242896 | tf_op jit(solution)/shard_map/all_gather | solution.py:112
  133.9 4.8 %fusion = f32[320]{0:T(512)S(1)} fusion(bf16[320,8192]{1,0:T(8,128)(2,1)} %all-gather.4.cloned.1.call-done, bf16[8192,128]{1,0:T(8,128)(2,1)} %all-gather.6.cloned.1.call-done, bf16[320,128]{1,0:T(8,128)(2,1)S(1)} %bitcast.50), kind=kOutput, calls=%fused_computation.7 | convolution fusion | flops 671211200 | bytes 7423232 | tf_op jit(solution)/shard_map/dot_general | solution.py:56
  138.7 59.9 %all-gather.8.cloned.1.call-done = bf16[8192,128]{1,0:T(8,128)(2,1)} async-done(((bf16[512,128]{1,0:T(8,128)(2,1)}), bf16[8192,128]{1,0:T(8,128)(2,1)}) %all-gather.8.cloned.1.call-update) | async-done | bytes 2097168 | tf_op jit(solution)/shard_map/all_gather | solution.py:63
  198.6 4.8 %fusion.1 = f32[320]{0:T(512)S(1)} fusion(bf16[320,8192]{1,0:T(8,128)(2,1)} %all-gather.4.cloned.1.call-done, bf16[8192,128]{1,0:T(8,128)(2,1)} %all-gather.8.cloned.1.call-done, bf16[320,128]{1,0:T(8,128)(2,1)S(1)} %bitcast.51), kind=kOutput, calls=%fused_computation.8 | convolution fusion | flops 671211200 | bytes 7423232 | tf_op jit(solution)/shard_map/dot_general | solution.py:61
  203.3 2.5 all-reduce.1
  206.1 39.4 %all-reduce = (f32[4]{0:T(128)S(1)}, f32[4]{0:T(128)S(1)}) all-reduce(f32[4]{0:T(128)S(1)} %get-tuple-element.7, f32[4]{0:T(128)S(1)} %get-tuple-element.8), channel_id=1, replica_groups=mesh['dp'=4,'mp'=2,'section'=4] {'dp','section'}, use_global_device_ids=true, to_apply=%region_7.8 | all-reduce | flops 8 | bytes 64 | tf_op jit(solution)/shard_map/psum | solution.py:39
  246.0 1.4 gather_fusion.1
  247.5 7.9 %all_to_all.15 = bf16[4,80,3]{1,2,0:T(4,128)(2,1)S(1)} all-to-all(bf16[4,80,3]{1,2,0:T(4,128)(2,1)S(1)} %broadcast_select_fusion.2), channel_id=1, replica_groups=mesh['dp'=4,'mp'=2,'section'=4] {'dp'}, dimensions={0} | all-to-all | bytes 3840 | tf_op jit(solution)/shard_map/all_to_all | solution.py:106
  255.6 6.5 %fusion.3 = f32[8192,128]{1,0:T(8,128)} fusion(bf16[320,8192]{1,0:T(8,128)(2,1)} %all-gather.4.cloned.1.call-done, bf16[320,128]{1,0:T(8,128)(2,1)S(1)} %bitcast.52, f32[320]{0:T(512)S(1)} %get-tuple-element.17), kind=kOutput, calls=%fused_computation.11 | convolution fusion | flops 671211520 | bytes 9520384 | tf_op jit(solution)/shard_map/dot_general | solution.py:80
  262.6 91.0 %reduce-scatter.2.cloned.1.call-done = f32[512,128]{1,0:T(8,128)} async-done(((f32[8192,128]{1,0:T(8,128)}), f32[512,128]{1,0:T(8,128)}) %reduce-scatter.2.cloned.1.call-update) | async-done | bytes 262160 | tf_op jit(solution)/shard_map/reduce_scatter | solution.py:79
  (52 shorter events, 4.4 us)
Async XLA Ops:
  7.2 5.4 %copy-start = (bf16[256,4096]{1,0:T(8,128)(2,1)S(1)}, bf16[256,4096]{1,0:T(8,128)(2,1)}, u32[]{:S(2)}) copy-start(bf16[256,4096]{1,0:T(8,128)(2,1)} %param.9) | copy-start | bytes 6291460
  19.9 72.4 %all-to-all-start = ((bf16[4,80,4096]{2,1,0:T(8,128)(2,1)}), bf16[4,80,4096]{2,1,0:T(8,128)(2,1)}, u32[]{:S(2)}, u32[]{:S(2)}) async-start(bf16[4,80,4096]{2,1,0:T(8,128)(2,1)} %broadcast_select_fusion), calls=%async_computation | async-start | bytes 5242880 | tf_op jit(solution)/shard_map/all_to_all | solution.py:104
  26.2 66.8 %copy-start.1 = (bf16[256,128]{1,0:T(8,128)(2,1)S(1)}, bf16[256,128]{1,0:T(8,128)(2,1)}, u32[]{:S(2)}) copy-start(bf16[256,128]{1,0:T(8,128)(2,1)} %param.10) | copy-start | bytes 196612
  26.2 72.4 %copy-start.2 = (bf16[4096]{0:T(1024)(128)(2,1)S(1)}, bf16[4096]{0:T(1024)(128)(2,1)}, u32[]{:S(2)}) copy-start(bf16[4096]{0:T(1024)(128)(2,1)} %param.15) | copy-start | bytes 24580
  26.2 72.4 %copy-start.5 = (bf16[256]{0:T(256)(128)(2,1)S(1)}, bf16[256]{0:T(256)(128)(2,1)}, u32[]{:S(2)}) copy-start(bf16[256]{0:T(256)(128)(2,1)} %param.11) | copy-start | bytes 1540
  26.2 92.2 %all-gather.6.cloned.1.call-start = ((), (), s32[]{:S(2)}) async-start(), calls=%async_computation.5 | async-start | bytes 2228224 | tf_op jit(solution)/shard_map/all_gather | solution.py:58
  27.0 106.9 %all-gather.4.cloned.1.call-start = ((), (), s32[]{:S(2)}) async-start(), calls=%async_computation.4 | async-start | bytes 7864320 | tf_op jit(solution)/shard_map/all_gather | solution.py:112
  92.3 7.0 %copy-start.4 = (s32[2]{0:T(128)S(1)}, s32[2]{0:T(128)}, u32[]{:S(2)}) copy-start(s32[2]{0:T(128)} %param.12) | copy-start | bytes 28
  92.3 106.3 %all-gather.8.cloned.1.call-start = ((), (), s32[]{:S(2)}) async-start(), calls=%async_computation.6 | async-start | bytes 2228224 | tf_op jit(solution)/shard_map/all_gather | solution.py:63
  95.2 9.2 %all-to-all-start.2 = ((bf16[4,80,128]{2,1,0:T(8,128)(2,1)}), bf16[4,80,128]{2,1,0:T(8,128)(2,1)S(1)}, u32[]{:S(2)}, u32[]{:S(2)}) async-start(bf16[4,80,128]{2,1,0:T(8,128)(2,1)} %broadcast_select_fusion.1), calls=%async_computation.2 | async-start | bytes 163840 | tf_op jit(solution)/shard_map/all_to_all | solution.py:105
  98.5 255.2 %reduce-scatter.2.cloned.1.call-start = ((), (), s32[]{:S(2)}) async-start(), calls=%async_computation.7 | async-start | bytes 4456448 | tf_op jit(solution)/shard_map/reduce_scatter | solution.py:79
  138.7 67.4 %copy-start.3 = (s32[2]{0:T(128)S(1)}, s32[2]{0:T(128)}, u32[]{:S(2)}) copy-start(s32[2]{0:T(128)} %param.13) | copy-start | bytes 28
Sparse Core Ops, SparseCore 0:
  29.8 88.5 all-gather.5
  120.0 13.8 all-gather.3
  136.7 61.8 all-gather.7
  262.2 91.4 reduce-scatter.1
where the time goes:
time: 361 us; the launch traced here: 360 us
  waiting for transfers between devices  252 us (70%)
  blocking collectives  49.8 us (14%)
  matrix products  16.7 us (5%)
  between operations  13.9 us (4%)
  starting transfers between devices  9.77 us (3%)
  local copies, waits for them, and re-layouts  9.48 us (3%)
  other arithmetic  8.41 us (2%)
    reduce_scatter x1, waiting for transfers between devices, weight_grads(): lax.psum_scatter(lax.dot_general(whole, change, (((0,), (0,)), ((), ())),...  91 us
    all_to_all x1, waiting for transfers between devices, body(): lax.all_to_all(send_states, 'dp', split_axis=0, concat_axis=0, tiled=True)  65.3 us
    all_gather x1, waiting for transfers between devices, project(): lax.all_gather(reference_k, ('dp', 'section'), axis=0, tiled=True)  59.9 us
    psum x1, blocking collectives, advantages(): lax.psum((jnp.sum(member * reward[:, None], axis=0), jnp.sum(member * (re...  39.4 us
    all_gather x1, waiting for transfers between devices, body(): whole = lax.all_gather(learn_states, 'mp', axis=1, tiled=True)  15.4 us
    all_gather x1, waiting for transfers between devices, project(): lax.all_gather(policy_k, ('dp', 'section'), axis=0, tiled=True)  14 us
    all_to_all x1, blocking collectives, body(): lax.all_to_all(send_extras, 'dp', split_axis=0, concat_axis=0, tiled=True)  7.91 us
  transfers between devices with their start and end apart: 6, of which 6 were waited for; matrix products, arithmetic and copies ran while one was open for 2% of the time, Pallas kernels for 0%

commit v1 on v0

v1 whole, which is shorter than its diff:
```python
import functools

import jax
import jax.numpy as jnp
from jax import lax
from jax.experimental import pallas as pl
from jax.experimental.pallas import tpu as pltpu
from jax.sharding import PartitionSpec as P

GROUP = 8
kl_weight = 0.4
var_offset = 0.25
F32 = jnp.float32
BF16 = jnp.bfloat16
MESH = pl.DeviceIdType.MESH
LAST = (((1,), (1,)), ((), ()))


def kernel(
    N, M, S, cap, width,
    states, dirs, old, lens, gids, routes, head, pol, ref,
    grad, pack,
    own, sbuf, ksend, kt, dbuf, msg1, msg2, rgl, tbuf, tsum, hot, chg, gsend, grecv, psend, precv,
    own_sem, s_send, s_recv, k_send, k_recv, d_send, d_recv, m1_send, m1_recv, m2_send, m2_recv,
    t_send, t_recv, g_send, g_recv, p_send, p_recv,
):
    z, m, s = lax.axis_index("dp"), lax.axis_index("mp"), lax.axis_index("section")
    per = N // M
    T = states.shape[0]
    nl = lens.shape[0]
    L = T // nl
    Q = S * nl
    F, C = pol.shape

    def at(zz, mm, ss):
        return {"dp": zz, "mp": mm, "section": ss}

    def remote(src, dst, send, recv, to):
        return pltpu.make_async_remote_copy(
            src_ref=src, dst_ref=dst, send_sem=send, recv_sem=recv, device_id=to, device_id_type=MESH
        )

    def landed(dst, sem):
        pltpu.make_async_copy(dst, dst, sem).wait()

    plane = [
        (k, (m + k % M) % M, (s + k // M) % S) for k in range(1, S * M)
    ]
    column = [((z + dz) % N, (m + dm) % M) for dz in range(1, N) for dm in range(M)]

    barrier = pltpu.get_barrier_semaphore()
    for _, mm, ss in plane:
        pl.semaphore_signal(barrier, inc=1, device_id=at(z, mm, ss), device_id_type=MESH)
    for zz, mm in column:
        pl.semaphore_signal(barrier, inc=1, device_id=at(zz, mm, s), device_id_type=MESH)

    own_copy = pltpu.make_async_copy(states, own, own_sem)
    own_copy.start()

    def columns(ii, ss):
        return states.at[:, pl.ds(pl.multiple_of((S * ii + ss) * F, F), F)]

    for ii in range(per):
        pltpu.make_async_copy(columns(ii, s), sbuf.at[ii, s], s_recv.at[ii, s]).start()
    ksend[0:C, :] = pol[...].astype(F32).T.astype(BF16)
    ksend[C : 2 * C, :] = ref[...].astype(F32).T.astype(BF16)
    dbuf[s, m] = dirs[...].astype(F32).T.astype(BF16)

    pl.semaphore_wait(barrier, S * M - 1 + (N - 1) * M)

    sent = []

    def go(copy):
        copy.start()
        sent.append(copy)

    for k, mm, ss in plane:
        go(remote(dbuf.at[s, m], dbuf.at[s, m], d_send.at[k], d_recv.at[s, m], at(z, mm, ss)))
    m_k = z // per
    k_slot = kt.at[z % per, m]
    k_sem = k_recv.at[z % per, m]
    order = [(ds, ii) for ii in range(per) for ds in range(1, S)]
    for n in range(max(len(order), N - 1)):
        if n < len(order):
            ds, ii = order[n]
            ss = (s + ds) % S
            go(remote(columns(ii, ss), sbuf.at[ii, s], s_send.at[ii, ds], s_recv.at[ii, s], at(z, m, ss)))
        if n < N - 1:
            dz = n + 1
            go(remote(ksend, k_slot, k_send.at[dz], k_sem, at((z + dz) % N, m_k, s)))
    k_near = remote(ksend, k_slot, k_send.at[0], k_sem, at(z, m_k, s))

    @pl.when(m_k != m)
    def _():
        k_near.start()

    @pl.when(m_k == m)
    def _():
        pltpu.make_async_copy(ksend, k_slot, k_sem).start()

    own_copy.wait()
    scores = lax.dot_general(
        jnp.broadcast_to(head[...], (16, head.shape[1])), own[...], LAST, preferred_element_type=F32
    )[0:1, :]
    spot = lax.broadcasted_iota(jnp.int32, (1, L), 1)
    for r in range(nl):
        mine = jnp.where(spot < lens[r], scores[:, r * L : (r + 1) * L], 0.0)
        msg1[s, m, r : r + 1, :] = jnp.broadcast_to(jnp.sum(mine, axis=1, keepdims=True), (1, 128))
        msg1[s, m, nl + r : nl + r + 1, :] = jnp.full((1, 128), lens[r].astype(F32))
        msg1[s, m, 2 * nl + r : 2 * nl + r + 1, :] = jnp.full((1, 128), gids[r].astype(F32))
    for k, mm, ss in plane:
        go(remote(msg1.at[s, m], msg1.at[s, m], m1_send.at[k], m1_recv.at[s, m], at(z, mm, ss)))

    rows = max(16, N)
    shard = lax.broadcasted_iota(jnp.int32, (rows, T), 0)
    choose = (shard == routes[...]).astype(F32)
    upto = (
        lax.broadcasted_iota(jnp.int32, (T, T), 0) <= lax.broadcasted_iota(jnp.int32, (T, T), 1)
    ).astype(F32).astype(BF16)
    ranked = jnp.dot(choose.astype(BF16), upto, preferred_element_type=F32) - 1.0
    within = jnp.sum(ranked * choose, axis=0, keepdims=True)
    slot = routes[...].astype(F32) * width + within + (z * cap).astype(F32)
    for r in range(N):
        place = lax.broadcasted_iota(jnp.int32, (width, T), 0).astype(F32) + float(r * width)
        hot[r * width : (r + 1) * width, :] = (place == slot).astype(F32).astype(BF16)

    for k, mm, ss in plane:
        landed(msg1.at[ss, mm], m1_recv.at[ss, mm])
    for t in range(S):
        total = msg1[t, 0, 0:nl, :]
        for mm in range(1, M):
            total = total + msg1[t, mm, 0:nl, :]
        rgl[0, t * nl : (t + 1) * nl, :] = total
        rgl[1, t * nl : (t + 1) * nl, :] = msg1[t, 0, nl : 2 * nl, :]
        rgl[2, t * nl : (t + 1) * nl, :] = msg1[t, 0, 2 * nl : 3 * nl, :]
    reward = rgl[0] / jnp.sqrt(rgl[1])
    lane = lax.broadcasted_iota(jnp.int32, (Q, 128), 1).astype(F32)
    member = rgl[2] == lane
    held = jnp.where(member, reward, 0.0)
    msg2[z, 0:1, :] = jnp.sum(held, axis=0, keepdims=True)
    msg2[z, 1:2, :] = jnp.sum(held * held, axis=0, keepdims=True)
    msg2[z, 2:8, :] = jnp.zeros((6, 128), F32)
    for dz in range(1, N):
        go(remote(msg2.at[z], msg2.at[z], m2_send.at[dz], m2_recv.at[z], at((z + dz) % N, m, s)))
    for dz in range(1, N):
        landed(msg2.at[(z + dz) % N], m2_recv.at[(z + dz) % N])
    sums = msg2[0]
    for zz in range(1, N):
        sums = sums + msg2[zz]
    center = sums[0:1, :] / GROUP
    spread = sums[1:2, :] / GROUP - center * center
    own_center = jnp.sum(jnp.where(member, center, 0.0), axis=1, keepdims=True)
    own_spread = jnp.sum(jnp.where(member, spread, 0.0), axis=1, keepdims=True)
    advantage = ((reward - own_center) / jnp.sqrt(own_spread + var_offset)).astype(BF16).astype(F32)
    valid = (
        lax.broadcasted_iota(jnp.int32, (Q, L), 1).astype(F32) < rgl[1][:, 0:1]
    ).astype(F32)

    for k, mm, ss in plane:
        landed(dbuf.at[ss, mm], d_recv.at[ss, mm])
    for ii in range(per):
        for mm in range(M):
            landed(kt.at[ii, mm], k_recv.at[ii, mm])

    for t in range(S):
        keys = None
        for ii in range(per):
            landed(sbuf.at[ii, t], s_recv.at[ii, t])
            part = lax.dot_general(
                kt[ii].reshape(2 * M * C, F), sbuf[ii, t], LAST, preferred_element_type=F32
            )
            keys = part if keys is None else keys + part
        for which in range(2):
            term = None
            for mm in range(M):
                low = (2 * mm + which) * C
                part = jnp.sum(dbuf[t, mm].astype(F32) * keys[low : low + C, :], axis=0, keepdims=True)
                term = part if term is None else term + part
            for r in range(nl):
                q = t * nl + r
                tbuf[s, m, which, q : q + 1, :] = term[:, r * L : (r + 1) * L]
    for k, mm, ss in plane:
        go(remote(tbuf.at[s, m], tbuf.at[s, m], t_send.at[k], t_recv.at[s, m], at(z, mm, ss)))
    for k, mm, ss in plane:
        landed(tbuf.at[ss, mm], t_recv.at[ss, mm])
    terms = None
    for t in range(S):
        for mm in range(M):
            terms = tbuf[t, mm] if terms is None else terms + tbuf[t, mm]
    tp, tr = terms[0], terms[1]
    coef = valid * (-advantage * jnp.exp(tp) + kl_weight * (1.0 - jnp.exp(tr - tp)))
    for q in range(Q):
        t, r = q // nl, q % nl
        for mm in range(M):
            chg[mm * C : (mm + 1) * C, q * L : (q + 1) * L] = (
                dbuf[t, mm, :, r * L : (r + 1) * L].astype(F32) * coef[q : q + 1, :]
            ).astype(BF16)
    g_near = []
    for ii in range(per):
        part = jnp.dot(chg[...], sbuf[ii].reshape(S * T, F), preferred_element_type=F32)
        for mm in range(M):
            gsend[ii, mm] = part[mm * C : (mm + 1) * C, :].astype(BF16)
        zz = m * per + ii
        for dm in range(1, M):
            mm = (m + dm) % M
            go(remote(gsend.at[ii, mm], grecv.at[z], g_send.at[ii, dm], g_recv.at[z], at(zz, mm, s)))
        far = remote(gsend.at[ii, m], grecv.at[z], g_send.at[ii, 0], g_recv.at[z], at(zz, m, s))
        g_near.append((zz, far))

        @pl.when(zz != z)
        def _(far=far):
            far.start()

        @pl.when(zz == z)
        def _(ii=ii):
            pltpu.make_async_copy(gsend.at[ii, m], grecv.at[z], g_recv.at[z]).start()

    tsum[...] = tp
    logp = old[...] + tsum[pl.ds(s * nl, nl), :]
    row = jnp.concatenate([logp[r : r + 1, :] for r in range(nl)], axis=1)
    high = row.astype(BF16).astype(F32)
    mid = (row - high).astype(BF16).astype(F32)
    low = row - high - mid
    split = jnp.concatenate([high, mid, low, jnp.zeros((13, T), F32)], axis=0).astype(BF16)
    placed = lax.dot_general(split, hot[...], LAST, preferred_element_type=F32)
    line = placed[0:1, :] + placed[1:2, :] + placed[2:3, :]
    for r in range(N):
        psend[r] = jnp.broadcast_to(line[:, r * width : (r + 1) * width], (8, width))
    for dz in range(1, N):
        zz = (z + dz) % N
        go(remote(psend.at[zz], precv.at[z], p_send.at[dz], p_recv.at[z], at(zz, m, s)))
    precv[z] = psend[z]
    for dz in range(1, N):
        landed(precv.at[(z + dz) % N], p_recv.at[(z + dz) % N])
    packed = precv[0]
    for zz in range(1, N):
        packed = packed + precv[zz]
    pack[0] = packed[0:1, : N * cap]

    total = None
    for zz in range(N):
        landed(grecv.at[zz], g_recv.at[zz])
        part = grecv[zz].astype(F32)
        total = part if total is None else total + part
    grad[...] = total.T

    for copy in sent:
        copy.wait_send()

    @pl.when(m_k != m)
    def _():
        k_near.wait_send()

    for zz, far in g_near:

        @pl.when(zz != z)
        def _(far=far):
            far.wait_send()


def body(states, direction, old_logp, lengths, group_ids, routes, reward_head, policy_k, reference_k):
    N, M, S = lax.axis_size("dp"), lax.axis_size("mp"), lax.axis_size("section")
    T = states.shape[0]
    nl = lengths.shape[0]
    L = T // nl
    F, C = policy_k.shape
    per = N // M
    Q = S * nl
    cap = max(2, 5 * T // (4 * N))
    width = -(-N * cap // 128) * 128
    vm = pl.BlockSpec(memory_space=pltpu.VMEM)
    sm = pl.BlockSpec(memory_space=pltpu.SMEM)
    dma = pltpu.SemaphoreType.DMA
    high = -(-3 * nl // 8) * 8
    grad_k, packed = pl.pallas_call(
        functools.partial(kernel, N, M, S, cap, width),
        out_shape=(
            jax.ShapeDtypeStruct((F, C), F32),
            jax.ShapeDtypeStruct((1, 1, N * cap), F32),
        ),
        in_specs=[pl.BlockSpec(memory_space=pl.ANY), vm, vm, sm, sm, vm, vm, vm, vm],
        out_specs=(vm, vm),
        scratch_shapes=[
            pltpu.VMEM(states.shape, BF16),
            pltpu.VMEM((per, S, T, F), BF16),
            pltpu.VMEM((2 * C, F), BF16),
            pltpu.VMEM((per, M, 2 * C, F), BF16),
            pltpu.VMEM((S, M, C, T), BF16),
            pltpu.VMEM((S, M, high, 128), F32),
            pltpu.VMEM((N, 8, 128), F32),
            pltpu.VMEM((3, Q, 128), F32),
            pltpu.VMEM((S, M, 2, Q, L), F32),
            pltpu.VMEM((Q, L), F32),
            pltpu.VMEM((N * width, T), BF16),
            pltpu.VMEM((M * C, S * T), BF16),
            pltpu.VMEM((per, M, C, F), BF16),
            pltpu.VMEM((N, C, F), BF16),
            pltpu.VMEM((N, 8, width), F32),
            pltpu.VMEM((N, 8, width), F32),
            dma,
            dma((per, S)), dma((per, S)),
            dma((N,)), dma((per, M)),
            dma((S * M,)), dma((S, M)),
            dma((S * M,)), dma((S, M)),
            dma((N,)), dma((N,)),
            dma((S * M,)), dma((S, M)),
            dma((per, M)), dma((N,)),
            dma((N,)), dma((N,)),
        ],
        compiler_params=pltpu.CompilerParams(
            collective_id=0, has_side_effects=True, vmem_limit_bytes=48 * 1024 * 1024
        ),
    )(
        states,
        direction,
        old_logp.astype(F32).reshape(nl, L),
        lengths,
        group_ids,
        routes.reshape(1, T),
        reward_head.reshape(1, -1),
        policy_k,
        reference_k,
    )
    return grad_k, packed


def solution(mesh):
    both = ("dp", "section")
    return jax.shard_map(
        body,
        mesh=mesh,
        in_specs=(
            P(both, "mp"),
            P(both, "mp"),
            P(both),
            P(both),
            P(both),
            P(both, None),
            P("mp"),
            P(both, "mp"),
            P(both, "mp"),
        ),
        out_specs=(P(both, "mp"), P("dp", "section", None)),
        check_vma=False,
    )
```

time: 361 us -> 73 us (0.20)
  waiting for transfers between devices: 252 us -> 0 us
  Pallas kernels: 0 us -> 63.2 us
  blocking collectives: 49.8 us -> 0 us
  matrix products: 16.7 us -> 0 us
  between operations: 13.9 us -> 0.66 us
  starting transfers between devices: 9.77 us -> 0 us
  other arithmetic: 8.41 us -> 0.66 us
    reduce_scatter x1 -> x0, waiting for transfers between devices: 91 us -> none  [weight_grads(): lax.psum_scatter(lax.dot_general(whole, change, (((0,), (0,)), ((), ())),...]
    all_gather x3 -> x0, waiting for transfers between devices: 89.4 us -> none  [the longest x1 59.9 us: project(): lax.all_gather(reference_k, ('dp', 'section'), axis=0, tiled=True)]
    all_to_all x2 -> x0, waiting for transfers between devices: 70.4 us -> none  [the longest x1 65.3 us: body(): lax.all_to_all(send_states, 'dp', split_axis=0, concat_axis=0, tiled=True)]
    pallas_call x0 -> x1, Pallas kernels: none -> 63.2 us  [body(): pl.pallas_call(functools.partial(kernel, N, M, S, cap, width), out_shape=...]
    psum x2 -> x0, blocking collectives: 41.9 us -> none  [the longest x1 39.4 us: advantages(): lax.psum((jnp.sum(member * reward[:, None], axis=0), jnp.sum(member * (re...]
    dot_general x4 -> x0, matrix products: 16.7 us -> none  [the longest x1 6.45 us: weight_grads(): lax.dot_general(whole, change, (((0,), (0,)), ((), ())), preferred_elemen...]
    all_to_all x2 -> x0, starting transfers between devices: 9.61 us -> none  [the longest x1 6.32 us: body(): lax.all_to_all(send_states, 'dp', split_axis=0, concat_axis=0, tiled=True)]
    all_to_all x1 -> x0, blocking collectives: 7.91 us -> none  [body(): lax.all_to_all(send_extras, 'dp', split_axis=0, concat_axis=0, tiled=True)]
  transfers between devices with their start and end apart: 6 -> 0, of which waited for: 6 -> 0; matrix products, arithmetic and copies ran while one was open for 2% -> 0% of each run, Pallas kernels for 0% -> 0%
where the time goes in v1:
time: 73 us; the launch traced here: 72.7 us
  Pallas kernels  63.2 us (87%)
  local copies, waits for them, and re-layouts  8.19 us (11%)
    pallas_call x1, Pallas kernels, body(): pl.pallas_call(functools.partial(kernel, N, M, S, cap, width), out_shape=...  63.2 us
    unnamed x16, local copies, waits for them, and re-layouts  7.49 us

profile of v1, /device:TPU:0, one launch (start us, length us, event | category | flops | bytes accessed | tf_op | source)
XLA Modules:
  0.0 72.7 jit_solution(1289003888213801011)
XLA Ops:
  0.6 0.7 bitcast_convert_fusion.old
  1.3 0.7 reshape.18.head
  2.0 0.0 copy-start
  2.0 1.6 %copy-done = bf16[256,4096]{1,0:T(8,128)(2,1)S(1)} copy-done((bf16[256,4096]{1,0:T(8,128)(2,1)S(1)}, bf16[256,4096]{1,0:T(8,128)(2,1)}, u32[]{:S(2)}) %copy-start) | copy-done | bytes 2097176
  3.6 0.0 copy-start.1
  3.6 0.9 %copy-done.1 = bf16[512,128]{1,0:T(8,128)(2,1)S(1)} copy-done((bf16[512,128]{1,0:T(8,128)(2,1)S(1)}, bf16[512,128]{1,0:T(8,128)(2,1)}, u32[]{:S(2)}) %copy-start.1) | copy-done | bytes 131096
  4.5 0.0 copy-start.2
  4.5 0.9 %copy-done.2 = bf16[512,128]{1,0:T(8,128)(2,1)S(1)} copy-done((bf16[512,128]{1,0:T(8,128)(2,1)S(1)}, bf16[512,128]{1,0:T(8,128)(2,1)}, u32[]{:S(2)}) %copy-start.2) | copy-done | bytes 131096
  5.4 0.0 copy-start.3
  5.4 0.8 %copy-done.3 = bf16[256,128]{1,0:T(8,128)(2,1)S(1)} copy-done((bf16[256,128]{1,0:T(8,128)(2,1)S(1)}, bf16[256,128]{1,0:T(8,128)(2,1)}, u32[]{:S(2)}) %copy-start.3) | copy-done | bytes 65560
  6.2 0.0 copy-start.4
  6.2 0.7 copy-done.4
  6.9 0.0 copy-start.5
  6.9 0.7 copy-done.5
  7.6 0.0 copy-start.6
  7.6 0.7 copy-done.6
  8.2 63.2 %shard_map.104 = (f32[512,128]{1,0:T(8,128)S(1)}, f32[1,1,320]{2,1,0:T(1,128)S(1)}) custom-call(bf16[256,4096]{1,0:T(8,128)(2,1)S(1)} %copy-done, bf16[256,128]{1,0:T(8,128)(2,1)S(1)} %copy-done.3, f32[2,128]{1,0:T(2,128)S(1)} %bitcast_convert_fusion.old, s32[2]{0:T(128)S(1)} %copy-done.5, s32[2]{0:T(128)S(1)} %copy-done.6, s32[1,256]{1,0:T(1,128)S(1)} %bitcast.4, ...), custom_call_target="tpu_custom_call" | custom-call | tf_op jit(solution)/shard_map/pallas_call | solution.py:275
  71.4 0.7 copy.13
  72.1 0.6 copy.14
Async XLA Ops:
  2.0 1.6 %copy-start = (bf16[256,4096]{1,0:T(8,128)(2,1)S(1)}, bf16[256,4096]{1,0:T(8,128)(2,1)}, u32[]{:S(2)}) copy-start(bf16[256,4096]{1,0:T(8,128)(2,1)} %states.1) | copy-start | bytes 6291460
  3.6 0.9 %copy-start.1 = (bf16[512,128]{1,0:T(8,128)(2,1)S(1)}, bf16[512,128]{1,0:T(8,128)(2,1)}, u32[]{:S(2)}) copy-start(bf16[512,128]{1,0:T(8,128)(2,1)} %pol.1) | copy-start | bytes 393220
  4.5 0.9 %copy-start.2 = (bf16[512,128]{1,0:T(8,128)(2,1)S(1)}, bf16[512,128]{1,0:T(8,128)(2,1)}, u32[]{:S(2)}) copy-start(bf16[512,128]{1,0:T(8,128)(2,1)} %ref.1) | copy-start | bytes 393220
  5.4 0.8 %copy-start.3 = (bf16[256,128]{1,0:T(8,128)(2,1)S(1)}, bf16[256,128]{1,0:T(8,128)(2,1)}, u32[]{:S(2)}) copy-start(bf16[256,128]{1,0:T(8,128)(2,1)} %dirs.1) | copy-start | bytes 196612
  6.2 0.7 copy-start.4
  6.9 0.7 copy-start.5
  7.6 0.7 copy-start.6

commit v2 on v1

--- a/solution.py
+++ b/solution.py
@@ -18,8 +18,9 @@
 
 def kernel(
     N, M, S, cap, width,
-    states, dirs, old, lens, gids, routes, head, pol, ref,
+    states, dirs_in, old_in, lens_in, gids_in, routes_in, head_in, pol_in, ref_in,
     grad, pack,
+    dirs, old, lens, gids, routes, head, pol, ref, in_sem,
     own, sbuf, ksend, kt, dbuf, msg1, msg2, rgl, tbuf, tsum, hot, chg, gsend, grecv, psend, precv,
     own_sem, s_send, s_recv, k_send, k_recv, d_send, d_recv, m1_send, m1_recv, m2_send, m2_recv,
     t_send, t_recv, g_send, g_recv, p_send, p_recv,
@@ -27,10 +28,10 @@
     z, m, s = lax.axis_index("dp"), lax.axis_index("mp"), lax.axis_index("section")
     per = N // M
     T = states.shape[0]
-    nl = lens.shape[0]
+    nl = lens_in.shape[0]
     L = T // nl
     Q = S * nl
-    F, C = pol.shape
+    F, C = pol_in.shape
 
     def at(zz, mm, ss):
         return {"dp": zz, "mp": mm, "section": ss}
@@ -54,6 +55,17 @@
     for zz, mm in column:
         pl.semaphore_signal(barrier, inc=1, device_id=at(zz, mm, s), device_id_type=MESH)
 
+    loads = [
+        pltpu.make_async_copy(src, dst, in_sem.at[n])
+        for n, (src, dst) in enumerate(
+            (
+                (dirs_in, dirs), (pol_in, pol), (ref_in, ref), (head_in, head),
+                (lens_in, lens), (gids_in, gids), (routes_in, routes), (old_in, old),
+            )
+        )
+    ]
+    for load in loads:
+        load.start()
     own_copy = pltpu.make_async_copy(states, own, own_sem)
     own_copy.start()
 
@@ -62,8 +74,7 @@
 
     for ii in range(per):
         pltpu.make_async_copy(columns(ii, s), sbuf.at[ii, s], s_recv.at[ii, s]).start()
-    ksend[0:C, :] = pol[...].astype(F32).T.astype(BF16)
-    ksend[C : 2 * C, :] = ref[...].astype(F32).T.astype(BF16)
+    loads[0].wait()
     dbuf[s, m] = dirs[...].astype(F32).T.astype(BF16)
 
     pl.semaphore_wait(barrier, S * M - 1 + (N - 1) * M)
@@ -74,20 +85,22 @@
         copy.start()
         sent.append(copy)
 
-    for k, mm, ss in plane:
-        go(remote(dbuf.at[s, m], dbuf.at[s, m], d_send.at[k], d_recv.at[s, m], at(z, mm, ss)))
+    for ds in range(1, S):
+        ss = (s + ds) % S
+        go(remote(dbuf.at[s, m], dbuf.at[s, m], d_send.at[0, ds], d_recv.at[s, m], at(z, m, ss)))
+    for ii in range(per):
+        for ds in range(1, S):
+            ss = (s + ds) % S
+            go(remote(columns(ii, ss), sbuf.at[ii, s], s_send.at[ii, ds], s_recv.at[ii, s], at(z, m, ss)))
+    for load in loads[1:3]:
+        load.wait()
+    ksend[0:C, :] = pol[...].astype(F32).T.astype(BF16)
+    ksend[C : 2 * C, :] = ref[...].astype(F32).T.astype(BF16)
     m_k = z // per
     k_slot = kt.at[z % per, m]
     k_sem = k_recv.at[z % per, m]
-    order = [(ds, ii) for ii in range(per) for ds in range(1, S)]
-    for n in range(max(len(order), N - 1)):
-        if n < len(order):
-            ds, ii = order[n]
-            ss = (s + ds) % S
-            go(remote(columns(ii, ss), sbuf.at[ii, s], s_send.at[ii, ds], s_recv.at[ii, s], at(z, m, ss)))
-        if n < N - 1:
-            dz = n + 1
-            go(remote(ksend, k_slot, k_send.at[dz], k_sem, at((z + dz) % N, m_k, s)))
+    for dz in range(1, N):
+        go(remote(ksend, k_slot, k_send.at[dz], k_sem, at((z + dz) % N, m_k, s)))
     k_near = remote(ksend, k_slot, k_send.at[0], k_sem, at(z, m_k, s))
 
     @pl.when(m_k != m)
@@ -98,9 +111,11 @@
     def _():
         pltpu.make_async_copy(ksend, k_slot, k_sem).start()
 
+    for load in loads[3:]:
+        load.wait()
     own_copy.wait()
     scores = lax.dot_general(
-        jnp.broadcast_to(head[...], (16, head.shape[1])), own[...], LAST, preferred_element_type=F32
+        jnp.broadcast_to(head[...].reshape(1, -1), (16, head.shape[0])), own[...], LAST, preferred_element_type=F32
     )[0:1, :]
     spot = lax.broadcasted_iota(jnp.int32, (1, L), 1)
     for r in range(nl):
@@ -110,6 +125,14 @@
         msg1[s, m, 2 * nl + r : 2 * nl + r + 1, :] = jnp.full((1, 128), gids[r].astype(F32))
     for k, mm, ss in plane:
         go(remote(msg1.at[s, m], msg1.at[s, m], m1_send.at[k], m1_recv.at[s, m], at(z, mm, ss)))
+
+    for ds in range(S):
+        ss = (s + ds) % S
+        if ds:
+            landed(dbuf.at[ss, m], d_recv.at[ss, m])
+        for dm in range(1, M):
+            to = at(z, (m + dm) % M, s)
+            go(remote(dbuf.at[ss, m], dbuf.at[ss, m], d_send.at[dm, ds], d_recv.at[ss, m], to))
 
     rows = max(16, N)
     shard = lax.broadcasted_iota(jnp.int32, (rows, T), 0)
@@ -156,13 +179,16 @@
         lax.broadcasted_iota(jnp.int32, (Q, L), 1).astype(F32) < rgl[1][:, 0:1]
     ).astype(F32)
 
-    for k, mm, ss in plane:
-        landed(dbuf.at[ss, mm], d_recv.at[ss, mm])
     for ii in range(per):
         for mm in range(M):
             landed(kt.at[ii, mm], k_recv.at[ii, mm])
-
-    for t in range(S):
+    for ds in range(S):
+        for dm in range(1, M):
+            ss, mm = (s + ds) % S, (m + dm) % M
+            landed(dbuf.at[ss, mm], d_recv.at[ss, mm])
+
+    for ds in range(S):
+        t = (s + ds) % S
         keys = None
         for ii in range(per):
             landed(sbuf.at[ii, t], s_recv.at[ii, t])
@@ -177,24 +203,29 @@
                 part = jnp.sum(dbuf[t, mm].astype(F32) * keys[low : low + C, :], axis=0, keepdims=True)
                 term = part if term is None else term + part
             for r in range(nl):
-                q = t * nl + r
-                tbuf[s, m, which, q : q + 1, :] = term[:, r * L : (r + 1) * L]
+                n = which * nl + r
+                tbuf[s, m, t, n : n + 1, :] = term[:, r * L : (r + 1) * L]
     for k, mm, ss in plane:
         go(remote(tbuf.at[s, m], tbuf.at[s, m], t_send.at[k], t_recv.at[s, m], at(z, mm, ss)))
     for k, mm, ss in plane:
         landed(tbuf.at[ss, mm], t_recv.at[ss, mm])
-    terms = None
     for t in range(S):
-        for mm in range(M):
-            terms = tbuf[t, mm] if terms is None else terms + tbuf[t, mm]
-    tp, tr = terms[0], terms[1]
-    coef = valid * (-advantage * jnp.exp(tp) + kl_weight * (1.0 - jnp.exp(tr - tp)))
-    for q in range(Q):
-        t, r = q // nl, q % nl
-        for mm in range(M):
-            chg[mm * C : (mm + 1) * C, q * L : (q + 1) * L] = (
-                dbuf[t, mm, :, r * L : (r + 1) * L].astype(F32) * coef[q : q + 1, :]
-            ).astype(BF16)
+        terms = None
+        for ss in range(S):
+            for mm in range(M):
+                terms = tbuf[ss, mm, t] if terms is None else terms + tbuf[ss, mm, t]
+        tp, tr = terms[0:nl, :], terms[nl : 2 * nl, :]
+        tsum[t] = tp
+        adv = advantage[t * nl : (t + 1) * nl, :]
+        coef = valid[t * nl : (t + 1) * nl, :] * (
+            -adv * jnp.exp(tp) + kl_weight * (1.0 - jnp.exp(tr - tp))
+        )
+        for r in range(nl):
+            q = t * nl + r
+            for mm in range(M):
+                chg[mm * C : (mm + 1) * C, q * L : (q + 1) * L] = (
+                    dbuf[t, mm, :, r * L : (r + 1) * L].astype(F32) * coef[r : r + 1, :]
+                ).astype(BF16)
     g_near = []
     for ii in range(per):
         part = jnp.dot(chg[...], sbuf[ii].reshape(S * T, F), preferred_element_type=F32)
@@ -215,27 +246,28 @@
         def _(ii=ii):
             pltpu.make_async_copy(gsend.at[ii, m], grecv.at[z], g_recv.at[z]).start()
 
-    tsum[...] = tp
-    logp = old[...] + tsum[pl.ds(s * nl, nl), :]
-    row = jnp.concatenate([logp[r : r + 1, :] for r in range(nl)], axis=1)
-    high = row.astype(BF16).astype(F32)
-    mid = (row - high).astype(BF16).astype(F32)
-    low = row - high - mid
-    split = jnp.concatenate([high, mid, low, jnp.zeros((13, T), F32)], axis=0).astype(BF16)
-    placed = lax.dot_general(split, hot[...], LAST, preferred_element_type=F32)
-    line = placed[0:1, :] + placed[1:2, :] + placed[2:3, :]
-    for r in range(N):
-        psend[r] = jnp.broadcast_to(line[:, r * width : (r + 1) * width], (8, width))
-    for dz in range(1, N):
-        zz = (z + dz) % N
-        go(remote(psend.at[zz], precv.at[z], p_send.at[dz], p_recv.at[z], at(zz, m, s)))
+        if ii == 0:
+            logp = tsum[s]
+            row = jnp.concatenate([logp[r : r + 1, :] for r in range(nl)], axis=1) + old[...].reshape(1, T).astype(F32)
+            high = row.astype(BF16).astype(F32)
+            mid = (row - high).astype(BF16).astype(F32)
+            low = row - high - mid
+            split = jnp.concatenate([high, mid, low, jnp.zeros((13, T), F32)], axis=0).astype(BF16)
+            placed = lax.dot_general(split, hot[...], LAST, preferred_element_type=F32)
+            line = placed[0:1, :] + placed[1:2, :] + placed[2:3, :]
+            for r in range(N):
+                psend[r] = line[:, r * width : (r + 1) * width]
+            for dz in range(1, N):
+                zz = (z + dz) % N
+                go(remote(psend.at[zz], precv.at[z], p_send.at[dz], p_recv.at[z], at(zz, m, s)))
+
     precv[z] = psend[z]
     for dz in range(1, N):
         landed(precv.at[(z + dz) % N], p_recv.at[(z + dz) % N])
     packed = precv[0]
     for zz in range(1, N):
         packed = packed + precv[zz]
-    pack[0] = packed[0:1, : N * cap]
+    pack[0] = packed[:, : N * cap]
 
     total = None
     for zz in range(N):
@@ -269,7 +301,6 @@
     cap = max(2, 5 * T // (4 * N))
     width = -(-N * cap // 128) * 128
     vm = pl.BlockSpec(memory_space=pltpu.VMEM)
-    sm = pl.BlockSpec(memory_space=pltpu.SMEM)
     dma = pltpu.SemaphoreType.DMA
     high = -(-3 * nl // 8) * 8
     grad_k, packed = pl.pallas_call(
@@ -278,9 +309,18 @@
             jax.ShapeDtypeStruct((F, C), F32),
             jax.ShapeDtypeStruct((1, 1, N * cap), F32),
         ),
-        in_specs=[pl.BlockSpec(memory_space=pl.ANY), vm, vm, sm, sm, vm, vm, vm, vm],
+        in_specs=[pl.BlockSpec(memory_space=pl.ANY)] * 9,
         out_specs=(vm, vm),
         scratch_shapes=[
+            pltpu.VMEM(direction.shape, BF16),
+            pltpu.VMEM((T,), BF16),
+            pltpu.SMEM((nl,), jnp.int32),
+            pltpu.SMEM((nl,), jnp.int32),
+            pltpu.VMEM((1, T), jnp.int32),
+            pltpu.VMEM(reward_head.shape, BF16),
+            pltpu.VMEM((F, C), BF16),
+            pltpu.VMEM((F, C), BF16),
+            dma((8,)),
             pltpu.VMEM(states.shape, BF16),
             pltpu.VMEM((per, S, T, F), BF16),
             pltpu.VMEM((2 * C, F), BF16),
@@ -289,18 +329,18 @@
             pltpu.VMEM((S, M, high, 128), F32),
             pltpu.VMEM((N, 8, 128), F32),
             pltpu.VMEM((3, Q, 128), F32),
-            pltpu.VMEM((S, M, 2, Q, L), F32),
-            pltpu.VMEM((Q, L), F32),
+            pltpu.VMEM((S, M, S, 2 * nl, L), F32),
+            pltpu.VMEM((S, nl, L), F32),
             pltpu.VMEM((N * width, T), BF16),
             pltpu.VMEM((M * C, S * T), BF16),
             pltpu.VMEM((per, M, C, F), BF16),
             pltpu.VMEM((N, C, F), BF16),
-            pltpu.VMEM((N, 8, width), F32),
-            pltpu.VMEM((N, 8, width), F32),
+            pltpu.VMEM((N, 1, width), F32),
+            pltpu.VMEM((N, 1, width), F32),
             dma,
             dma((per, S)), dma((per, S)),
             dma((N,)), dma((per, M)),
-            dma((S * M,)), dma((S, M)),
+            dma((M, S)), dma((S, M)),
             dma((S * M,)), dma((S, M)),
             dma((N,)), dma((N,)),
             dma((S * M,)), dma((S, M)),
@@ -308,16 +348,16 @@
             dma((N,)), dma((N,)),
         ],
         compiler_params=pltpu.CompilerParams(
-            collective_id=0, has_side_effects=True, vmem_limit_bytes=48 * 1024 * 1024
+            collective_id=0, has_side_effects=True, vmem_limit_bytes=64 * 1024 * 1024
         ),
     )(
         states,
         direction,
-        old_logp.astype(F32).reshape(nl, L),
+        old_logp,
         lengths,
         group_ids,
         routes.reshape(1, T),
-        reward_head.reshape(1, -1),
+        reward_head,
         policy_k,
         reference_k,
     )

time: 73 us -> 60.9 us (0.83)
  Pallas kernels: 63.2 us -> 56.7 us
  local copies, waits for them, and re-layouts: 8.19 us -> 2.9 us
    pallas_call x1, Pallas kernels: 63.2 us -> 56.7 us  [body(): pl.pallas_call(functools.partial(kernel, N, M, S, cap, width), out_shape=...]
    unnamed x16 -> x2, local copies, waits for them, and re-layouts: 7.49 us -> 2.9 us
where the time goes in v2:
time: 60.9 us; the launch traced here: 60.2 us
  Pallas kernels  56.7 us (93%)
  local copies, waits for them, and re-layouts  2.9 us (5%)
  between operations  0.64 us (1%)
    pallas_call x1, Pallas kernels, body(): pl.pallas_call(functools.partial(kernel, N, M, S, cap, width), out_shape=...  56.7 us
    unnamed x2, local copies, waits for them, and re-layouts  2.9 us

profile of v2, /device:TPU:0, one launch (start us, length us, event | category | flops | bytes accessed | tf_op | source)
XLA Modules:
  0.0 60.2 jit_solution(2030025373573150046)
XLA Ops:
  0.6 56.7 %shard_map.104 = (f32[512,128]{1,0:T(8,128)}, f32[1,1,320]{2,1,0:T(1,128)}) custom-call(bf16[256,4096]{1,0:T(8,128)(2,1)} %states.1, bf16[256,128]{1,0:T(8,128)(2,1)} %dirs_in.1, bf16[256]{0:T(256)(128)(2,1)} %old_in.1, s32[2]{0:T(128)} %lens_in.1, s32[2]{0:T(128)} %gids_in.1, s32[1,256]{1,0:T(1,128)} %bitcast.1, bf16[4096]{0:T(1024)(128)(2,1)} %head_in.1, ...), custom_call_target="tpu_custom_call" | custom-call | tf_op jit(solution)/shard_map/pallas_call | solution.py:306
  57.3 1.7 %copy.13 = f32[512,128]{1,0:T(8,128)} copy(f32[512,128]{1,0:T(8,128)} %get-tuple-element.4) | data formatting | bytes 524288
  59.0 1.2 %copy.14 = f32[1,1,320]{2,1,0:T(1,128)} copy(f32[1,1,320]{2,1,0:T(1,128)} %get-tuple-element.5) | data formatting | bytes 2560

commit v3 on v2

--- a/solution.py
+++ b/solution.py
@@ -22,7 +22,7 @@
     grad, pack,
     dirs, old, lens, gids, routes, head, pol, ref, in_sem,
     own, sbuf, ksend, kt, dbuf, msg1, msg2, rgl, tbuf, tsum, hot, chg, gsend, grecv, psend, precv,
-    own_sem, s_send, s_recv, k_send, k_recv, d_send, d_recv, m1_send, m1_recv, m2_send, m2_recv,
+    own_sem, s_send, s_recv, k_send, k_recv, k_fwd, d_send, d_recv, m1_send, m1_recv, m2_send, m2_recv,
     t_send, t_recv, g_send, g_recv, p_send, p_recv,
 ):
     z, m, s = lax.axis_index("dp"), lax.axis_index("mp"), lax.axis_index("section")
@@ -48,6 +48,16 @@
         (k, (m + k % M) % M, (s + k // M) % S) for k in range(1, S * M)
     ]
     column = [((z + dz) % N, (m + dm) % M) for dz in range(1, N) for dm in range(M)]
+
+    def mate(k):
+        if S & (S - 1):
+            return (s + k) % S
+        at_s, bit = s, 1
+        while bit < S:
+            if k & bit:
+                at_s = at_s + bit - 2 * bit * ((s // bit) % 2)
+            bit *= 2
+        return at_s
 
     barrier = pltpu.get_barrier_semaphore()
     for _, mm, ss in plane:
@@ -86,11 +96,10 @@
         sent.append(copy)
 
     for ds in range(1, S):
-        ss = (s + ds) % S
-        go(remote(dbuf.at[s, m], dbuf.at[s, m], d_send.at[0, ds], d_recv.at[s, m], at(z, m, ss)))
-    for ii in range(per):
-        for ds in range(1, S):
-            ss = (s + ds) % S
+        go(remote(dbuf.at[s, m], dbuf.at[s, m], d_send.at[0, ds], d_recv.at[s, m], at(z, m, mate(ds))))
+    for ds in range(1, S):
+        ss = mate(ds)
+        for ii in range(per):
             go(remote(columns(ii, ss), sbuf.at[ii, s], s_send.at[ii, ds], s_recv.at[ii, s], at(z, m, ss)))
     for load in loads[1:3]:
         load.wait()
@@ -99,8 +108,32 @@
     m_k = z // per
     k_slot = kt.at[z % per, m]
     k_sem = k_recv.at[z % per, m]
-    for dz in range(1, N):
-        go(remote(ksend, k_slot, k_send.at[dz], k_sem, at((z + dz) % N, m_k, s)))
+    k_out = []
+    for n, step in enumerate((1, -1)):
+        inside = (z + step >= 0) & (z + step < N)
+        copy = remote(ksend, k_slot, k_send.at[n + 1], k_sem, at((z + step + N) % N, m_k, s))
+        k_out.append((inside, copy))
+
+        @pl.when(inside)
+        def _(copy=copy):
+            copy.start()
+
+    def onward(d):
+        for step in (1, -1):
+            i = z - step * d
+            ii = (i + N) % per
+            held_here = (i >= m * per) & (i < (m + 1) * per)
+            to = z + step
+
+            @pl.when(held_here & (to >= 0) & (to < N))
+            def _(ii=ii, to=to):
+                for mm in range(M):
+                    part = kt.at[ii, mm]
+                    landed(part, k_recv.at[ii, mm])
+                    remote(
+                        part, part, k_fwd.at[ii, mm], k_recv.at[ii, mm], at((to + N) % N, m, s)
+                    ).start()
+
     k_near = remote(ksend, k_slot, k_send.at[0], k_sem, at(z, m_k, s))
 
     @pl.when(m_k != m)
@@ -127,26 +160,14 @@
         go(remote(msg1.at[s, m], msg1.at[s, m], m1_send.at[k], m1_recv.at[s, m], at(z, mm, ss)))
 
     for ds in range(S):
-        ss = (s + ds) % S
+        ss = mate(ds)
         if ds:
             landed(dbuf.at[ss, m], d_recv.at[ss, m])
         for dm in range(1, M):
             to = at(z, (m + dm) % M, s)
             go(remote(dbuf.at[ss, m], dbuf.at[ss, m], d_send.at[dm, ds], d_recv.at[ss, m], to))
 
-    rows = max(16, N)
-    shard = lax.broadcasted_iota(jnp.int32, (rows, T), 0)
-    choose = (shard == routes[...]).astype(F32)
-    upto = (
-        lax.broadcasted_iota(jnp.int32, (T, T), 0) <= lax.broadcasted_iota(jnp.int32, (T, T), 1)
-    ).astype(F32).astype(BF16)
-    ranked = jnp.dot(choose.astype(BF16), upto, preferred_element_type=F32) - 1.0
-    within = jnp.sum(ranked * choose, axis=0, keepdims=True)
-    slot = routes[...].astype(F32) * width + within + (z * cap).astype(F32)
-    for r in range(N):
-        place = lax.broadcasted_iota(jnp.int32, (width, T), 0).astype(F32) + float(r * width)
-        hot[r * width : (r + 1) * width, :] = (place == slot).astype(F32).astype(BF16)
-
+    onward(1)
     for k, mm, ss in plane:
         landed(msg1.at[ss, mm], m1_recv.at[ss, mm])
     for t in range(S):
@@ -165,6 +186,22 @@
     msg2[z, 2:8, :] = jnp.zeros((6, 128), F32)
     for dz in range(1, N):
         go(remote(msg2.at[z], msg2.at[z], m2_send.at[dz], m2_recv.at[z], at((z + dz) % N, m, s)))
+
+    rows = max(16, N)
+    shard = lax.broadcasted_iota(jnp.int32, (rows, T), 0)
+    choose = (shard == routes[...]).astype(F32)
+    upto = (
+        lax.broadcasted_iota(jnp.int32, (T, T), 0) <= lax.broadcasted_iota(jnp.int32, (T, T), 1)
+    ).astype(F32).astype(BF16)
+    ranked = jnp.dot(choose.astype(BF16), upto, preferred_element_type=F32) - 1.0
+    within = jnp.sum(ranked * choose, axis=0, keepdims=True)
+    slot = routes[...].astype(F32) * width + within + (z * cap).astype(F32)
+    for r in range(N):
+        place = lax.broadcasted_iota(jnp.int32, (width, T), 0).astype(F32) + float(r * width)
+        hot[r * width : (r + 1) * width, :] = (place == slot).astype(F32).astype(BF16)
+
+    for d in range(2, N - 1):
+        onward(d)
     for dz in range(1, N):
         landed(msg2.at[(z + dz) % N], m2_recv.at[(z + dz) % N])
     sums = msg2[0]
@@ -179,16 +216,23 @@
         lax.broadcasted_iota(jnp.int32, (Q, L), 1).astype(F32) < rgl[1][:, 0:1]
     ).astype(F32)
 
+    k_passed = []
     for ii in range(per):
-        for mm in range(M):
-            landed(kt.at[ii, mm], k_recv.at[ii, mm])
+        i = m * per + ii
+        k_passed.append(((i < z) & (z < N - 1)) | ((i > z) & (z > 0)))
+
+        @pl.when(jnp.logical_not(k_passed[ii]))
+        def _(ii=ii):
+            for mm in range(M):
+                landed(kt.at[ii, mm], k_recv.at[ii, mm])
+
     for ds in range(S):
         for dm in range(1, M):
-            ss, mm = (s + ds) % S, (m + dm) % M
+            ss, mm = mate(ds), (m + dm) % M
             landed(dbuf.at[ss, mm], d_recv.at[ss, mm])
 
     for ds in range(S):
-        t = (s + ds) % S
+        t = mate(ds)
         keys = None
         for ii in range(per):
             landed(sbuf.at[ii, t], s_recv.at[ii, t])
@@ -283,6 +327,20 @@
     def _():
         k_near.wait_send()
 
+    for inside, copy in k_out:
+
+        @pl.when(inside)
+        def _(copy=copy):
+            copy.wait_send()
+
+    for ii in range(per):
+
+        @pl.when(k_passed[ii])
+        def _(ii=ii):
+            for mm in range(M):
+                part = kt.at[ii, mm]
+                remote(part, part, k_fwd.at[ii, mm], k_recv.at[ii, mm], at(z, m, s)).wait_send()
+
     for zz, far in g_near:
 
         @pl.when(zz != z)
@@ -309,7 +367,7 @@
             jax.ShapeDtypeStruct((F, C), F32),
             jax.ShapeDtypeStruct((1, 1, N * cap), F32),
         ),
-        in_specs=[pl.BlockSpec(memory_space=pl.ANY)] * 9,
+        in_specs=[pl.BlockSpec(memory_space=pltpu.HBM)] * 9,
         out_specs=(vm, vm),
         scratch_shapes=[
             pltpu.VMEM(direction.shape, BF16),
@@ -339,7 +397,7 @@
             pltpu.VMEM((N, 1, width), F32),
             dma,
             dma((per, S)), dma((per, S)),
-            dma((N,)), dma((per, M)),
+            dma((3,)), dma((per, M)), dma((per, M)),
             dma((M, S)), dma((S, M)),
             dma((S * M,)), dma((S, M)),
             dma((N,)), dma((N,)),
@@ -348,19 +406,14 @@
             dma((N,)), dma((N,)),
         ],
         compiler_params=pltpu.CompilerParams(
-            collective_id=0, has_side_effects=True, vmem_limit_bytes=64 * 1024 * 1024
+            collective_id=0, has_side_effects=True, vmem_limit_bytes=40 * 1024 * 1024
         ),
-    )(
-        states,
-        direction,
-        old_logp,
-        lengths,
-        group_ids,
-        routes.reshape(1, T),
-        reward_head,
-        policy_k,
-        reference_k,
-    )
+    )(*(
+        pltpu.with_memory_space_constraint(operand, pltpu.HBM)
+        for operand in (
+            states, direction, old_logp, lengths, group_ids, routes.reshape(1, T), reward_head, policy_k, reference_k
+        )
+    ))
     return grad_k, packed
 
 

time: 60.9 us -> 60.7 us (level)
  Pallas kernels: 56.7 us -> 58.4 us
  local copies, waits for them, and re-layouts: 2.9 us -> 1.27 us
    pallas_call x1, Pallas kernels: 56.7 us -> 58.4 us  [body(): pl.pallas_call(functools.partial(kernel, N, M, S, cap, width), out_shape=...]
    unnamed x2, local copies, waits for them, and re-layouts: 2.9 us -> 1.27 us
where the time goes in v3:
time: 60.7 us; the launch traced here: 60.3 us
  Pallas kernels  58.4 us (96%)
  local copies, waits for them, and re-layouts  1.27 us (2%)
  between operations  0.64 us (1%)
    pallas_call x1, Pallas kernels, body(): pl.pallas_call(functools.partial(kernel, N, M, S, cap, width), out_shape=...  58.4 us
    unnamed x2, local copies, waits for them, and re-layouts  1.27 us

profile of v3, /device:TPU:0, one launch (start us, length us, event | category | flops | bytes accessed | tf_op | source)
XLA Modules:
  0.0 60.3 jit_solution(15557493506520394827)
XLA Ops:
  0.6 58.4 %shard_map.104 = (f32[512,128]{1,0:T(8,128)S(1)}, f32[1,1,320]{2,1,0:T(1,128)S(1)}) custom-call(bf16[256,4096]{1,0:T(8,128)(2,1)} %states.1, bf16[256,128]{1,0:T(8,128)(2,1)} %dirs_in.1, bf16[256]{0:T(256)(128)(2,1)} %old_in.1, s32[2]{0:T(128)} %lens_in.1, s32[2]{0:T(128)} %gids_in.1, s32[1,256]{1,0:T(1,128)} %bitcast.1, bf16[4096]{0:T(1024)(128)(2,1)} %head_in.1, ...), custom_call_target="tpu_custom_call" | custom-call | tf_op jit(solution)/shard_map/pallas_call | solution.py:364
  59.0 0.7 %copy.13 = f32[512,128]{1,0:T(8,128)} copy(f32[512,128]{1,0:T(8,128)S(1)} %get-tuple-element.4) | data formatting | bytes 524288
  59.7 0.6 copy.14

commit v4 on v3

--- a/solution.py
+++ b/solution.py
@@ -21,9 +21,9 @@
     states, dirs_in, old_in, lens_in, gids_in, routes_in, head_in, pol_in, ref_in,
     grad, pack,
     dirs, old, lens, gids, routes, head, pol, ref, in_sem,
-    own, sbuf, ksend, kt, dbuf, msg1, msg2, rgl, tbuf, tsum, hot, chg, gsend, grecv, psend, precv,
+    own, sbuf, ksend, kt, dbuf, msg1, msg2, rgl, tbuf, tsum, hot, chg, gsend, gkeep, crecv, grecv, psend, precv,
     own_sem, s_send, s_recv, k_send, k_recv, k_fwd, d_send, d_recv, m1_send, m1_recv, m2_send, m2_recv,
-    t_send, t_recv, g_send, g_recv, p_send, p_recv,
+    t_send, t_recv, c_send, c_recv, g_send, g_recv, gate, p_send, p_recv,
 ):
     z, m, s = lax.axis_index("dp"), lax.axis_index("mp"), lax.axis_index("section")
     per = N // M
@@ -83,8 +83,15 @@
         return states.at[:, pl.ds(pl.multiple_of((S * ii + ss) * F, F), F)]
 
     for ii in range(per):
-        pltpu.make_async_copy(columns(ii, s), sbuf.at[ii, s], s_recv.at[ii, s]).start()
-    loads[0].wait()
+        for h in range(2):
+            rows = pl.ds(h * (T // 2), T // 2)
+            pltpu.make_async_copy(
+                columns(ii, s).at[rows], sbuf.at[ii, s, rows], s_recv.at[h, ii, s]
+            ).start()
+    for load in loads[0:3]:
+        load.wait()
+    ksend[0:C, :] = pol[...].astype(F32).T.astype(BF16)
+    ksend[C : 2 * C, :] = ref[...].astype(F32).T.astype(BF16)
     dbuf[s, m] = dirs[...].astype(F32).T.astype(BF16)
 
     pl.semaphore_wait(barrier, S * M - 1 + (N - 1) * M)
@@ -97,26 +104,43 @@
 
     for ds in range(1, S):
         go(remote(dbuf.at[s, m], dbuf.at[s, m], d_send.at[0, ds], d_recv.at[s, m], at(z, m, mate(ds))))
-    for ds in range(1, S):
-        ss = mate(ds)
-        for ii in range(per):
-            go(remote(columns(ii, ss), sbuf.at[ii, s], s_send.at[ii, ds], s_recv.at[ii, s], at(z, m, ss)))
-    for load in loads[1:3]:
-        load.wait()
-    ksend[0:C, :] = pol[...].astype(F32).T.astype(BF16)
-    ksend[C : 2 * C, :] = ref[...].astype(F32).T.astype(BF16)
     m_k = z // per
     k_slot = kt.at[z % per, m]
     k_sem = k_recv.at[z % per, m]
     k_out = []
-    for n, step in enumerate((1, -1)):
+
+    def send_keys(h, step):
         inside = (z + step >= 0) & (z + step < N)
-        copy = remote(ksend, k_slot, k_send.at[n + 1], k_sem, at((z + step + N) % N, m_k, s))
+        half = pl.ds(h * C, C)
+        sem = k_send.at[len(k_out)]
+        copy = remote(ksend.at[half], k_slot.at[half], sem, k_sem, at((z + step + N) % N, m_k, s))
         k_out.append((inside, copy))
 
         @pl.when(inside)
-        def _(copy=copy):
+        def _():
             copy.start()
+
+    turn = m % 2
+    mates = [mate(ds) for ds in range(1, S)]
+    if S > 2:
+        first, second = mates[0], mates[1]
+        mates[0] = first + turn * (second - first)
+        mates[1] = second + turn * (first - second)
+    for h in range(2):
+        rows = pl.ds(h * (T // 2), T // 2)
+        for ii in range(per):
+            if ii < 2:
+                send_keys(h, 1 - 2 * ii)
+            for n, ss in enumerate(mates):
+                go(
+                    remote(
+                        columns(ii, ss).at[rows],
+                        sbuf.at[ii, s, rows],
+                        s_send.at[h, ii, n],
+                        s_recv.at[h, ii, s],
+                        at(z, m, ss),
+                    )
+                )
 
     def onward(d):
         for step in (1, -1):
@@ -134,7 +158,7 @@
                         part, part, k_fwd.at[ii, mm], k_recv.at[ii, mm], at((to + N) % N, m, s)
                     ).start()
 
-    k_near = remote(ksend, k_slot, k_send.at[0], k_sem, at(z, m_k, s))
+    k_near = remote(ksend, k_slot, k_send.at[4], k_sem, at(z, m_k, s))
 
     @pl.when(m_k != m)
     def _():
@@ -235,7 +259,8 @@
         t = mate(ds)
         keys = None
         for ii in range(per):
-            landed(sbuf.at[ii, t], s_recv.at[ii, t])
+            for h in range(2):
+                landed(sbuf.at[ii, t, pl.ds(h * (T // 2), T // 2)], s_recv.at[h, ii, t])
             part = lax.dot_general(
                 kt[ii].reshape(2 * M * C, F), sbuf[ii, t], LAST, preferred_element_type=F32
             )
@@ -270,40 +295,71 @@
                 chg[mm * C : (mm + 1) * C, q * L : (q + 1) * L] = (
                     dbuf[t, mm, :, r * L : (r + 1) * L].astype(F32) * coef[r : r + 1, :]
                 ).astype(BF16)
-    g_near = []
-    for ii in range(per):
-        part = jnp.dot(chg[...], sbuf[ii].reshape(S * T, F), preferred_element_type=F32)
+    pair, odd = z // 2, z % 2
+    partner = z + 1 - 2 * odd
+    far = m != pair
+    near = m == pair
+    part = jnp.dot(chg[...], sbuf[1 - odd].reshape(S * T, F), preferred_element_type=F32)
+    for mm in range(M):
+        gsend[0, mm] = part[mm * C : (mm + 1) * C, :].astype(BF16)
+
+    def to_partner(mm):
+        return remote(gsend.at[0, mm], crecv.at[mm], c_send.at[mm], c_recv.at[mm], at(partner, m, s))
+
+    def to_owner(mm):
+        return remote(gsend.at[1, mm], grecv.at[pair], g_send.at[mm], g_recv.at[pair], at(2 * m + odd, mm, s))
+
+    def to_mate(mm):
+        return remote(gsend.at[0, mm], grecv.at[N // 2], c_send.at[mm], g_recv.at[N // 2], at(partner, mm, s))
+
+    def to_core(dm):
+        mm = (m + dm) % M
+        return remote(gsend.at[1, mm], grecv.at[pair], g_send.at[dm], g_recv.at[pair], at(z, mm, s))
+
+    @pl.when(far)
+    def _():
         for mm in range(M):
-            gsend[ii, mm] = part[mm * C : (mm + 1) * C, :].astype(BF16)
-        zz = m * per + ii
+            to_partner(mm).start()
+
+    part = jnp.dot(chg[...], sbuf[odd].reshape(S * T, F), preferred_element_type=F32)
+    for mm in range(M):
+        gkeep[mm] = part[mm * C : (mm + 1) * C, :]
+        gsend[1, mm] = part[mm * C : (mm + 1) * C, :].astype(BF16)
+
+    @pl.when(near)
+    def _():
         for dm in range(1, M):
-            mm = (m + dm) % M
-            go(remote(gsend.at[ii, mm], grecv.at[z], g_send.at[ii, dm], g_recv.at[z], at(zz, mm, s)))
-        far = remote(gsend.at[ii, m], grecv.at[z], g_send.at[ii, 0], g_recv.at[z], at(zz, m, s))
-        g_near.append((zz, far))
-
-        @pl.when(zz != z)
-        def _(far=far):
-            far.start()
-
-        @pl.when(zz == z)
-        def _(ii=ii):
-            pltpu.make_async_copy(gsend.at[ii, m], grecv.at[z], g_recv.at[z]).start()
-
-        if ii == 0:
-            logp = tsum[s]
-            row = jnp.concatenate([logp[r : r + 1, :] for r in range(nl)], axis=1) + old[...].reshape(1, T).astype(F32)
-            high = row.astype(BF16).astype(F32)
-            mid = (row - high).astype(BF16).astype(F32)
-            low = row - high - mid
-            split = jnp.concatenate([high, mid, low, jnp.zeros((13, T), F32)], axis=0).astype(BF16)
-            placed = lax.dot_general(split, hot[...], LAST, preferred_element_type=F32)
-            line = placed[0:1, :] + placed[1:2, :] + placed[2:3, :]
-            for r in range(N):
-                psend[r] = line[:, r * width : (r + 1) * width]
-            for dz in range(1, N):
-                zz = (z + dz) % N
-                go(remote(psend.at[zz], precv.at[z], p_send.at[dz], p_recv.at[z], at(zz, m, s)))
+            to_core(dm).start()
+        pltpu.make_async_copy(gsend.at[1, m], grecv.at[pair], g_recv.at[pair]).start()
+
+    logp = tsum[s]
+    row = jnp.concatenate([logp[r : r + 1, :] for r in range(nl)], axis=1) + old[...].reshape(1, T).astype(F32)
+    high = row.astype(BF16).astype(F32)
+    mid = (row - high).astype(BF16).astype(F32)
+    low = row - high - mid
+    split = jnp.concatenate([high, mid, low, jnp.zeros((13, T), F32)], axis=0).astype(BF16)
+    placed = lax.dot_general(split, hot[...], LAST, preferred_element_type=F32)
+    line = placed[0:1, :] + placed[1:2, :] + placed[2:3, :]
+    for r in range(N):
+        psend[r] = line[:, r * width : (r + 1) * width]
+    for dz in range(1, N):
+        zz = (z + dz) % N
+        go(remote(psend.at[zz], precv.at[z], p_send.at[dz], p_recv.at[z], at(zz, m, s)))
+
+
+    @pl.when(far)
+    def _():
+        for mm in range(M):
+            landed(crecv.at[mm], c_recv.at[mm])
+            gsend[1, mm] = (gkeep[mm] + crecv[mm].astype(F32)).astype(BF16)
+            to_owner(mm).start()
+        pl.semaphore_signal(gate, inc=1, device_id=at(z, pair, s), device_id_type=MESH)
+
+    @pl.when(near)
+    def _():
+        pl.semaphore_wait(gate, M - 1)
+        for mm in range(M):
+            to_mate(mm).start()
 
     precv[z] = psend[z]
     for dz in range(1, N):
@@ -314,7 +370,7 @@
     pack[0] = packed[:, : N * cap]
 
     total = None
-    for zz in range(N):
+    for zz in range(N // 2 + 1):
         landed(grecv.at[zz], g_recv.at[zz])
         part = grecv[zz].astype(F32)
         total = part if total is None else total + part
@@ -341,11 +397,18 @@
                 part = kt.at[ii, mm]
                 remote(part, part, k_fwd.at[ii, mm], k_recv.at[ii, mm], at(z, m, s)).wait_send()
 
-    for zz, far in g_near:
-
-        @pl.when(zz != z)
-        def _(far=far):
-            far.wait_send()
+    @pl.when(far)
+    def _():
+        for mm in range(M):
+            to_partner(mm).wait_send()
+            to_owner(mm).wait_send()
+
+    @pl.when(near)
+    def _():
+        for mm in range(M):
+            to_mate(mm).wait_send()
+        for dm in range(1, M):
+            to_core(dm).wait_send()
 
 
 def body(states, direction, old_logp, lengths, group_ids, routes, reward_head, policy_k, reference_k):
@@ -392,17 +455,21 @@
             pltpu.VMEM((N * width, T), BF16),
             pltpu.VMEM((M * C, S * T), BF16),
             pltpu.VMEM((per, M, C, F), BF16),
-            pltpu.VMEM((N, C, F), BF16),
+            pltpu.VMEM((M, C, F), F32),
+            pltpu.VMEM((M, C, F), BF16),
+            pltpu.VMEM((N // 2 + 1, C, F), BF16),
             pltpu.VMEM((N, 1, width), F32),
             pltpu.VMEM((N, 1, width), F32),
             dma,
-            dma((per, S)), dma((per, S)),
-            dma((3,)), dma((per, M)), dma((per, M)),
+            dma((2, per, S)), dma((2, per, S)),
+            dma((5,)), dma((per, M)), dma((per, M)),
             dma((M, S)), dma((S, M)),
             dma((S * M,)), dma((S, M)),
             dma((N,)), dma((N,)),
             dma((S * M,)), dma((S, M)),
-            dma((per, M)), dma((N,)),
+            dma((M,)), dma((M,)),
+            dma((M,)), dma((N // 2 + 1,)),
+            pltpu.SemaphoreType.REGULAR,
             dma((N,)), dma((N,)),
         ],
         compiler_params=pltpu.CompilerParams(

time: 60.7 us -> 65 us (1.071)
  Pallas kernels: 58.4 us -> 62.2 us
    pallas_call x1, Pallas kernels: 58.4 us -> 62.2 us  [body(): pl.pallas_call(functools.partial(kernel, N, M, S, cap, width), out_shape=...]
where the time goes in v4:
time: 65 us; the launch traced here: 64.1 us
  Pallas kernels  62.2 us (96%)
  local copies, waits for them, and re-layouts  1.27 us (2%)
    pallas_call x1, Pallas kernels, body(): pl.pallas_call(functools.partial(kernel, N, M, S, cap, width), out_shape=...  62.2 us

profile of v4, /device:TPU:0, one launch (start us, length us, event | category | flops | bytes accessed | tf_op | source)
XLA Modules:
  0.0 64.1 jit_solution(12429096297014048512)
XLA Ops:
  0.6 62.2 %shard_map.104 = (f32[512,128]{1,0:T(8,128)S(1)}, f32[1,1,320]{2,1,0:T(1,128)S(1)}) custom-call(bf16[256,4096]{1,0:T(8,128)(2,1)} %states.1, bf16[256,128]{1,0:T(8,128)(2,1)} %dirs_in.1, bf16[256]{0:T(256)(128)(2,1)} %old_in.1, s32[2]{0:T(128)} %lens_in.1, s32[2]{0:T(128)} %gids_in.1, s32[1,256]{1,0:T(1,128)} %bitcast.1, bf16[4096]{0:T(1024)(128)(2,1)} %head_in.1, ...), custom_call_target="tpu_custom_call" | custom-call | tf_op jit(solution)/shard_map/pallas_call | solution.py:427
  62.8 0.7 %copy.13 = f32[512,128]{1,0:T(8,128)} copy(f32[512,128]{1,0:T(8,128)S(1)} %get-tuple-element.4) | data formatting | bytes 524288
  63.5 0.6 copy.14

commit v5 on v2

--- a/solution.py
+++ b/solution.py
@@ -134,19 +134,6 @@
             to = at(z, (m + dm) % M, s)
             go(remote(dbuf.at[ss, m], dbuf.at[ss, m], d_send.at[dm, ds], d_recv.at[ss, m], to))
 
-    rows = max(16, N)
-    shard = lax.broadcasted_iota(jnp.int32, (rows, T), 0)
-    choose = (shard == routes[...]).astype(F32)
-    upto = (
-        lax.broadcasted_iota(jnp.int32, (T, T), 0) <= lax.broadcasted_iota(jnp.int32, (T, T), 1)
-    ).astype(F32).astype(BF16)
-    ranked = jnp.dot(choose.astype(BF16), upto, preferred_element_type=F32) - 1.0
-    within = jnp.sum(ranked * choose, axis=0, keepdims=True)
-    slot = routes[...].astype(F32) * width + within + (z * cap).astype(F32)
-    for r in range(N):
-        place = lax.broadcasted_iota(jnp.int32, (width, T), 0).astype(F32) + float(r * width)
-        hot[r * width : (r + 1) * width, :] = (place == slot).astype(F32).astype(BF16)
-
     for k, mm, ss in plane:
         landed(msg1.at[ss, mm], m1_recv.at[ss, mm])
     for t in range(S):
@@ -187,7 +174,8 @@
             ss, mm = (s + ds) % S, (m + dm) % M
             landed(dbuf.at[ss, mm], d_recv.at[ss, mm])
 
-    for ds in range(S):
+    @pl.loop(0, S)
+    def _(ds):
         t = (s + ds) % S
         keys = None
         for ii in range(per):
@@ -205,6 +193,7 @@
             for r in range(nl):
                 n = which * nl + r
                 tbuf[s, m, t, n : n + 1, :] = term[:, r * L : (r + 1) * L]
+
     for k, mm, ss in plane:
         go(remote(tbuf.at[s, m], tbuf.at[s, m], t_send.at[k], t_recv.at[s, m], at(z, mm, ss)))
     for k, mm, ss in plane:
@@ -246,20 +235,32 @@
         def _(ii=ii):
             pltpu.make_async_copy(gsend.at[ii, m], grecv.at[z], g_recv.at[z]).start()
 
-        if ii == 0:
-            logp = tsum[s]
-            row = jnp.concatenate([logp[r : r + 1, :] for r in range(nl)], axis=1) + old[...].reshape(1, T).astype(F32)
-            high = row.astype(BF16).astype(F32)
-            mid = (row - high).astype(BF16).astype(F32)
-            low = row - high - mid
-            split = jnp.concatenate([high, mid, low, jnp.zeros((13, T), F32)], axis=0).astype(BF16)
-            placed = lax.dot_general(split, hot[...], LAST, preferred_element_type=F32)
-            line = placed[0:1, :] + placed[1:2, :] + placed[2:3, :]
-            for r in range(N):
-                psend[r] = line[:, r * width : (r + 1) * width]
-            for dz in range(1, N):
-                zz = (z + dz) % N
-                go(remote(psend.at[zz], precv.at[z], p_send.at[dz], p_recv.at[z], at(zz, m, s)))
+    rows = max(16, N)
+    shard = lax.broadcasted_iota(jnp.int32, (rows, T), 0)
+    choose = (shard == routes[...]).astype(F32)
+    upto = (
+        lax.broadcasted_iota(jnp.int32, (T, T), 0) <= lax.broadcasted_iota(jnp.int32, (T, T), 1)
+    ).astype(F32).astype(BF16)
+    ranked = jnp.dot(choose.astype(BF16), upto, preferred_element_type=F32) - 1.0
+    within = jnp.sum(ranked * choose, axis=0, keepdims=True)
+    slot = routes[...].astype(F32) * width + within + (z * cap).astype(F32)
+    for r in range(N):
+        place = lax.broadcasted_iota(jnp.int32, (width, T), 0).astype(F32) + float(r * width)
+        hot[r * width : (r + 1) * width, :] = (place == slot).astype(F32).astype(BF16)
+
+    logp = tsum[s]
+    row = jnp.concatenate([logp[r : r + 1, :] for r in range(nl)], axis=1) + old[...].reshape(1, T).astype(F32)
+    high = row.astype(BF16).astype(F32)
+    mid = (row - high).astype(BF16).astype(F32)
+    low = row - high - mid
+    split = jnp.concatenate([high, mid, low, jnp.zeros((13, T), F32)], axis=0).astype(BF16)
+    placed = lax.dot_general(split, hot[...], LAST, preferred_element_type=F32)
+    line = placed[0:1, :] + placed[1:2, :] + placed[2:3, :]
+    for r in range(N):
+        psend[r] = line[:, r * width : (r + 1) * width]
+    for dz in range(1, N):
+        zz = (z + dz) % N
+        go(remote(psend.at[zz], precv.at[z], p_send.at[dz], p_recv.at[z], at(zz, m, s)))
 
     precv[z] = psend[z]
     for dz in range(1, N):
@@ -309,7 +310,7 @@
             jax.ShapeDtypeStruct((F, C), F32),
             jax.ShapeDtypeStruct((1, 1, N * cap), F32),
         ),
-        in_specs=[pl.BlockSpec(memory_space=pl.ANY)] * 9,
+        in_specs=[pl.BlockSpec(memory_space=pltpu.HBM)] * 9,
         out_specs=(vm, vm),
         scratch_shapes=[
             pltpu.VMEM(direction.shape, BF16),
@@ -348,19 +349,14 @@
             dma((N,)), dma((N,)),
         ],
         compiler_params=pltpu.CompilerParams(
-            collective_id=0, has_side_effects=True, vmem_limit_bytes=64 * 1024 * 1024
+            collective_id=0, has_side_effects=True, vmem_limit_bytes=40 * 1024 * 1024
         ),
-    )(
-        states,
-        direction,
-        old_logp,
-        lengths,
-        group_ids,
-        routes.reshape(1, T),
-        reward_head,
-        policy_k,
-        reference_k,
-    )
+    )(*(
+        pltpu.with_memory_space_constraint(operand, pltpu.HBM)
+        for operand in (
+            states, direction, old_logp, lengths, group_ids, routes.reshape(1, T), reward_head, policy_k, reference_k
+        )
+    ))
     return grad_k, packed
 
 

time: 60.9 us -> 60.1 us (0.987)
  local copies, waits for them, and re-layouts: 2.9 us -> 1.27 us
  Pallas kernels: 56.7 us -> 58.1 us
    unnamed x2, local copies, waits for them, and re-layouts: 2.9 us -> 1.27 us
    pallas_call x1, Pallas kernels: 56.7 us -> 58.1 us  [body(): pl.pallas_call(functools.partial(kernel, N, M, S, cap, width), out_shape=...]
where the time goes in v5:
time: 60.1 us; the launch traced here: 60 us
  Pallas kernels  58.1 us (97%)
  local copies, waits for them, and re-layouts  1.27 us (2%)
  between operations  0.64 us (1%)
    pallas_call x1, Pallas kernels, body(): pl.pallas_call(functools.partial(kernel, N, M, S, cap, width), out_shape=...  58.1 us
    unnamed x2, local copies, waits for them, and re-layouts  1.27 us

profile of v5, /device:TPU:0, one launch (start us, length us, event | category | flops | bytes accessed | tf_op | source)
XLA Modules:
  0.0 60.0 jit_solution(9037657223752261714)
XLA Ops:
  0.6 58.1 %shard_map.104 = (f32[512,128]{1,0:T(8,128)S(1)}, f32[1,1,320]{2,1,0:T(1,128)S(1)}) custom-call(bf16[256,4096]{1,0:T(8,128)(2,1)} %states.1, bf16[256,128]{1,0:T(8,128)(2,1)} %dirs_in.1, bf16[256]{0:T(256)(128)(2,1)} %old_in.1, s32[2]{0:T(128)} %lens_in.1, s32[2]{0:T(128)} %gids_in.1, s32[1,256]{1,0:T(1,128)} %bitcast.1, bf16[4096]{0:T(1024)(128)(2,1)} %head_in.1, ...), custom_call_target="tpu_custom_call" | custom-call | tf_op jit(solution)/shard_map/pallas_call | solution.py:307
  58.7 0.7 %copy.13 = f32[512,128]{1,0:T(8,128)} copy(f32[512,128]{1,0:T(8,128)S(1)} %get-tuple-element.4) | data formatting | bytes 524288
  59.4 0.6 copy.14

commit v6 on v5

--- a/solution.py
+++ b/solution.py
@@ -74,7 +74,10 @@
 
     for ii in range(per):
         pltpu.make_async_copy(columns(ii, s), sbuf.at[ii, s], s_recv.at[ii, s]).start()
-    loads[0].wait()
+    for load in loads[0:3]:
+        load.wait()
+    ksend[0:C, :] = pol[...].astype(F32).T.astype(BF16)
+    ksend[C : 2 * C, :] = ref[...].astype(F32).T.astype(BF16)
     dbuf[s, m] = dirs[...].astype(F32).T.astype(BF16)
 
     pl.semaphore_wait(barrier, S * M - 1 + (N - 1) * M)
@@ -88,19 +91,18 @@
     for ds in range(1, S):
         ss = (s + ds) % S
         go(remote(dbuf.at[s, m], dbuf.at[s, m], d_send.at[0, ds], d_recv.at[s, m], at(z, m, ss)))
-    for ii in range(per):
-        for ds in range(1, S):
-            ss = (s + ds) % S
-            go(remote(columns(ii, ss), sbuf.at[ii, s], s_send.at[ii, ds], s_recv.at[ii, s], at(z, m, ss)))
-    for load in loads[1:3]:
-        load.wait()
-    ksend[0:C, :] = pol[...].astype(F32).T.astype(BF16)
-    ksend[C : 2 * C, :] = ref[...].astype(F32).T.astype(BF16)
     m_k = z // per
     k_slot = kt.at[z % per, m]
     k_sem = k_recv.at[z % per, m]
-    for dz in range(1, N):
-        go(remote(ksend, k_slot, k_send.at[dz], k_sem, at((z + dz) % N, m_k, s)))
+    order = [(ds, ii) for ii in range(per) for ds in range(1, S)]
+    for n in range(max(len(order), 3 * (N - 1))):
+        if n % 3 == 0 and n // 3 < N - 1:
+            dz = n // 3 + 1
+            go(remote(ksend, k_slot, k_send.at[dz], k_sem, at((z + dz) % N, m_k, s)))
+        if n < len(order):
+            ds, ii = order[n]
+            ss = (s + 1 + (ds - 1 + m % 2) % max(1, S - 1)) % S
+            go(remote(columns(ii, ss), sbuf.at[ii, s], s_send.at[ii, ds], s_recv.at[ii, s], at(z, m, ss)))
     k_near = remote(ksend, k_slot, k_send.at[0], k_sem, at(z, m_k, s))
 
     @pl.when(m_k != m)
@@ -133,6 +135,19 @@
         for dm in range(1, M):
             to = at(z, (m + dm) % M, s)
             go(remote(dbuf.at[ss, m], dbuf.at[ss, m], d_send.at[dm, ds], d_recv.at[ss, m], to))
+
+    rows = max(16, N)
+    shard = lax.broadcasted_iota(jnp.int32, (rows, T), 0)
+    choose = (shard == routes[...]).astype(F32)
+    upto = (
+        lax.broadcasted_iota(jnp.int32, (T, T), 0) <= lax.broadcasted_iota(jnp.int32, (T, T), 1)
+    ).astype(F32).astype(BF16)
+    ranked = jnp.dot(choose.astype(BF16), upto, preferred_element_type=F32) - 1.0
+    within = jnp.sum(ranked * choose, axis=0, keepdims=True)
+    slot = routes[...].astype(F32) * width + within + (z * cap).astype(F32)
+    for r in range(N):
+        place = lax.broadcasted_iota(jnp.int32, (width, T), 0).astype(F32) + float(r * width)
+        hot[r * width : (r + 1) * width, :] = (place == slot).astype(F32).astype(BF16)
 
     for k, mm, ss in plane:
         landed(msg1.at[ss, mm], m1_recv.at[ss, mm])
@@ -203,51 +218,7 @@
         for ss in range(S):
             for mm in range(M):
                 terms = tbuf[ss, mm, t] if terms is None else terms + tbuf[ss, mm, t]
-        tp, tr = terms[0:nl, :], terms[nl : 2 * nl, :]
-        tsum[t] = tp
-        adv = advantage[t * nl : (t + 1) * nl, :]
-        coef = valid[t * nl : (t + 1) * nl, :] * (
-            -adv * jnp.exp(tp) + kl_weight * (1.0 - jnp.exp(tr - tp))
-        )
-        for r in range(nl):
-            q = t * nl + r
-            for mm in range(M):
-                chg[mm * C : (mm + 1) * C, q * L : (q + 1) * L] = (
-                    dbuf[t, mm, :, r * L : (r + 1) * L].astype(F32) * coef[r : r + 1, :]
-                ).astype(BF16)
-    g_near = []
-    for ii in range(per):
-        part = jnp.dot(chg[...], sbuf[ii].reshape(S * T, F), preferred_element_type=F32)
-        for mm in range(M):
-            gsend[ii, mm] = part[mm * C : (mm + 1) * C, :].astype(BF16)
-        zz = m * per + ii
-        for dm in range(1, M):
-            mm = (m + dm) % M
-            go(remote(gsend.at[ii, mm], grecv.at[z], g_send.at[ii, dm], g_recv.at[z], at(zz, mm, s)))
-        far = remote(gsend.at[ii, m], grecv.at[z], g_send.at[ii, 0], g_recv.at[z], at(zz, m, s))
-        g_near.append((zz, far))
-
-        @pl.when(zz != z)
-        def _(far=far):
-            far.start()
-
-        @pl.when(zz == z)
-        def _(ii=ii):
-            pltpu.make_async_copy(gsend.at[ii, m], grecv.at[z], g_recv.at[z]).start()
-
-    rows = max(16, N)
-    shard = lax.broadcasted_iota(jnp.int32, (rows, T), 0)
-    choose = (shard == routes[...]).astype(F32)
-    upto = (
-        lax.broadcasted_iota(jnp.int32, (T, T), 0) <= lax.broadcasted_iota(jnp.int32, (T, T), 1)
-    ).astype(F32).astype(BF16)
-    ranked = jnp.dot(choose.astype(BF16), upto, preferred_element_type=F32) - 1.0
-    within = jnp.sum(ranked * choose, axis=0, keepdims=True)
-    slot = routes[...].astype(F32) * width + within + (z * cap).astype(F32)
-    for r in range(N):
-        place = lax.broadcasted_iota(jnp.int32, (width, T), 0).astype(F32) + float(r * width)
-        hot[r * width : (r + 1) * width, :] = (place == slot).astype(F32).astype(BF16)
-
+        tsum[t] = terms
     logp = tsum[s]
     row = jnp.concatenate([logp[r : r + 1, :] for r in range(nl)], axis=1) + old[...].reshape(1, T).astype(F32)
     high = row.astype(BF16).astype(F32)
@@ -261,6 +232,40 @@
     for dz in range(1, N):
         zz = (z + dz) % N
         go(remote(psend.at[zz], precv.at[z], p_send.at[dz], p_recv.at[z], at(zz, m, s)))
+
+    for t in range(S):
+        tp, tr = tsum[t, 0:nl, :], tsum[t, nl : 2 * nl, :]
+        adv = advantage[t * nl : (t + 1) * nl, :]
+        coef = valid[t * nl : (t + 1) * nl, :] * (
+            -adv * jnp.exp(tp) + kl_weight * (1.0 - jnp.exp(tr - tp))
+        )
+        for r in range(nl):
+            q = t * nl + r
+            for mm in range(M):
+                chg[mm * C : (mm + 1) * C, q * L : (q + 1) * L] = (
+                    dbuf[t, mm, :, r * L : (r + 1) * L].astype(F32) * coef[r : r + 1, :]
+                ).astype(BF16)
+    g_near = []
+    above = (m > z // per).astype(jnp.int32)
+    for n in range(per):
+        ii = n + above * (per - 1 - 2 * n)
+        part = jnp.dot(chg[...], sbuf[ii].reshape(S * T, F), preferred_element_type=F32)
+        for mm in range(M):
+            gsend[ii, mm] = part[mm * C : (mm + 1) * C, :].astype(BF16)
+        zz = m * per + ii
+        for dm in range(1, M):
+            mm = (m + dm) % M
+            go(remote(gsend.at[ii, mm], grecv.at[z], g_send.at[ii, dm], g_recv.at[z], at(zz, mm, s)))
+        far = remote(gsend.at[ii, m], grecv.at[z], g_send.at[ii, 0], g_recv.at[z], at(zz, m, s))
+        g_near.append((zz, far))
+
+        @pl.when(zz != z)
+        def _(far=far):
+            far.start()
+
+        @pl.when(zz == z)
+        def _(ii=ii):
+            pltpu.make_async_copy(gsend.at[ii, m], grecv.at[z], g_recv.at[z]).start()
 
     precv[z] = psend[z]
     for dz in range(1, N):
@@ -331,7 +336,7 @@
             pltpu.VMEM((N, 8, 128), F32),
             pltpu.VMEM((3, Q, 128), F32),
             pltpu.VMEM((S, M, S, 2 * nl, L), F32),
-            pltpu.VMEM((S, nl, L), F32),
+            pltpu.VMEM((S, 2 * nl, L), F32),
             pltpu.VMEM((N * width, T), BF16),
             pltpu.VMEM((M * C, S * T), BF16),
             pltpu.VMEM((per, M, C, F), BF16),

time: 60.1 us -> 57.8 us (0.962)
  Pallas kernels: 58.1 us -> 55.2 us
    pallas_call x1, Pallas kernels: 58.1 us -> 55.2 us  [body(): pl.pallas_call(functools.partial(kernel, N, M, S, cap, width), out_shape=...]
where the time goes in v6:
time: 57.8 us; the launch traced here: 57.1 us
  Pallas kernels  55.2 us (96%)
  local copies, waits for them, and re-layouts  1.27 us (2%)
  between operations  0.64 us (1%)
    pallas_call x1, Pallas kernels, body(): pl.pallas_call(functools.partial(kernel, N, M, S, cap, width), out_shape=...  55.2 us
    unnamed x2, local copies, waits for them, and re-layouts  1.27 us

profile of v6, /device:TPU:0, one launch (start us, length us, event | category | flops | bytes accessed | tf_op | source)
XLA Modules:
  0.0 57.1 jit_solution(8121658039695643606)
XLA Ops:
  0.6 55.2 %shard_map.104 = (f32[512,128]{1,0:T(8,128)S(1)}, f32[1,1,320]{2,1,0:T(1,128)S(1)}) custom-call(bf16[256,4096]{1,0:T(8,128)(2,1)} %states.1, bf16[256,128]{1,0:T(8,128)(2,1)} %dirs_in.1, bf16[256]{0:T(256)(128)(2,1)} %old_in.1, s32[2]{0:T(128)} %lens_in.1, s32[2]{0:T(128)} %gids_in.1, s32[1,256]{1,0:T(1,128)} %bitcast.1, bf16[4096]{0:T(1024)(128)(2,1)} %head_in.1, ...), custom_call_target="tpu_custom_call" | custom-call | tf_op jit(solution)/shard_map/pallas_call | solution.py:312
  55.9 0.7 %copy.13 = f32[512,128]{1,0:T(8,128)} copy(f32[512,128]{1,0:T(8,128)S(1)} %get-tuple-element.4) | data formatting | bytes 524288
  56.6 0.6 copy.14

commit v7 on v6

--- a/solution.py
+++ b/solution.py
@@ -74,10 +74,7 @@
 
     for ii in range(per):
         pltpu.make_async_copy(columns(ii, s), sbuf.at[ii, s], s_recv.at[ii, s]).start()
-    for load in loads[0:3]:
-        load.wait()
-    ksend[0:C, :] = pol[...].astype(F32).T.astype(BF16)
-    ksend[C : 2 * C, :] = ref[...].astype(F32).T.astype(BF16)
+    loads[0].wait()
     dbuf[s, m] = dirs[...].astype(F32).T.astype(BF16)
 
     pl.semaphore_wait(barrier, S * M - 1 + (N - 1) * M)
@@ -95,9 +92,14 @@
     k_slot = kt.at[z % per, m]
     k_sem = k_recv.at[z % per, m]
     order = [(ds, ii) for ii in range(per) for ds in range(1, S)]
-    for n in range(max(len(order), 3 * (N - 1))):
-        if n % 3 == 0 and n // 3 < N - 1:
-            dz = n // 3 + 1
+    for n in range(max(len(order), S - 1 + N - 1)):
+        if n == S - 1:
+            for load in loads[1:3]:
+                load.wait()
+            ksend[0:C, :] = pol[...].astype(F32).T.astype(BF16)
+            ksend[C : 2 * C, :] = ref[...].astype(F32).T.astype(BF16)
+        if n >= S - 1 and n - (S - 1) < N - 1:
+            dz = n - (S - 1) + 1
             go(remote(ksend, k_slot, k_send.at[dz], k_sem, at((z + dz) % N, m_k, s)))
         if n < len(order):
             ds, ii = order[n]
@@ -191,7 +193,8 @@
 
     @pl.loop(0, S)
     def _(ds):
-        t = (s + ds) % S
+        near_by = 1 + (ds + S - 2 + m % 2) % max(1, S - 1)
+        t = (s + S - near_by * ((ds + S - 1) // S)) % S
         keys = None
         for ii in range(per):
             landed(sbuf.at[ii, t], s_recv.at[ii, t])

time: 57.8 us -> 57.9 us (level)
  no operation moved by 1% of the time
where the time goes in v7:
time: 57.9 us; the launch traced here: 57.2 us
  Pallas kernels  55.3 us (96%)
  local copies, waits for them, and re-layouts  1.27 us (2%)
  between operations  0.64 us (1%)
    pallas_call x1, Pallas kernels, body(): pl.pallas_call(functools.partial(kernel, N, M, S, cap, width), out_shape=...  55.3 us
    unnamed x2, local copies, waits for them, and re-layouts  1.27 us

profile of v7, /device:TPU:0, one launch (start us, length us, event | category | flops | bytes accessed | tf_op | source)
XLA Modules:
  0.0 57.2 jit_solution(11691294857133246042)
XLA Ops:
  0.6 55.3 %shard_map.104 = (f32[512,128]{1,0:T(8,128)S(1)}, f32[1,1,320]{2,1,0:T(1,128)S(1)}) custom-call(bf16[256,4096]{1,0:T(8,128)(2,1)} %states.1, bf16[256,128]{1,0:T(8,128)(2,1)} %dirs_in.1, bf16[256]{0:T(256)(128)(2,1)} %old_in.1, s32[2]{0:T(128)} %lens_in.1, s32[2]{0:T(128)} %gids_in.1, s32[1,256]{1,0:T(1,128)} %bitcast.1, bf16[4096]{0:T(1024)(128)(2,1)} %head_in.1, ...), custom_call_target="tpu_custom_call" | custom-call | tf_op jit(solution)/shard_map/pallas_call | solution.py:315
  55.9 0.7 %copy.13 = f32[512,128]{1,0:T(8,128)} copy(f32[512,128]{1,0:T(8,128)S(1)} %get-tuple-element.4) | data formatting | bytes 524288
  56.6 0.6 copy.14
